TPU v7x, 512 devices: a whole 4x8x8 slice. The times are simulated.
512 devices in a mesh: gx: 8 (over y), gy: 8 (over z), gz: 8 (over x, core).
Axes of the slice: x: 4, y: 8, z: 8, core: 2. Of those that a mesh axis runs over, the one named last changes fastest.
Arguments:
- coarse_density: float32 [64, 128, 512], P('gx', 'gy', 'gz'), may hold values from -6 to 6
- start_potential: float32 [128, 256, 1024], P('gx', 'gy', 'gz'), may hold values from -6 to 6
- pair_density: float32 [8192, 91], P(('gx', 'gy', 'gz')), may hold values from -6 to 6
- expansion: float32 [91, 9], replicated, may hold values from -0.625 to 0.625
- box_corners: int32 [8192, 3], P(('gx', 'gy', 'gz')), may hold values from 0 to 1023, as said below
- box_offsets: float32 [8192, 3], P(('gx', 'gy', 'gz')), may hold values from -0.5 to 0.5
- atom_lists: int32 [512, 44], P(('gx', 'gy', 'gz')), may hold values from 0 to 8191, as said below
- atom_counts: int32 [512], P(('gx', 'gy', 'gz')), may hold values from 16 to 44
Outputs:
- total_density: float32 [128, 256, 1024], P('gx', 'gy', 'gz')
- potential: float32 [128, 256, 1024], P('gx', 'gy', 'gz')
Inputs may be any that keep to these rules, and one draw needn't show every extreme that they name: `box_corners`: atom dom * 16 + j belongs to domain dom. Its box of 12 cells along each dimension starts inside that domain; either it crosses the domain's three upper faces or it lies within the domain. `atom_lists`: row d lists, in no particular order, every atom whose box meets domain d: the domain's own 16 atoms and the crossing atoms of its lower neighbours along x, y, z and the diagonals; a domain has at most 4 crossing atoms. Entries past atom_counts[d] are 0.
All inputs are finite; a program needn't handle non-finite values.
Results may differ from a plain program's by a relative error of at most 0.0003.
Values sent between devices are 32-bit elements; how exact they have to be, the bound alone decides.
A program may use at most 128 MiB of HBM per device.

v0:
```python
import jax
import jax.numpy as jnp
from jax import lax
from jax.sharding import PartitionSpec as P

BOX = 12
LEVELS = 5
CYCLES = 2
COARSE_SWEEPS = 4


RELAX = 0.8
INV_RC = 0.5
EXPONENTS = (
    (0, 0, 0),
    (1, 0, 0),
    (0, 1, 0),
    (0, 0, 1),
    (1, 1, 0),
    (0, 1, 1),
    (1, 0, 1),
    (2, 0, 0),
    (0, 2, 0),
    (0, 0, 2),
)


def with_halo(block, sides, width):
    for axis, dim in sides:
        count = lax.axis_size(axis)
        forward = [(i, i + 1) for i in range(count - 1)]
        backward = [(target, source) for source, target in forward]
        low = lax.ppermute(
            lax.slice_in_dim(block, block.shape[dim] - width, None, axis=dim), axis, forward
        )
        high = lax.ppermute(lax.slice_in_dim(block, 0, width, axis=dim), axis, backward)
        block = jnp.concatenate([low, block, high], axis=dim)
    return block


def shifted(value, axis, steps):
    count = lax.axis_size(axis)
    first, last = (max(0, -steps), min(count, count - steps))
    return lax.ppermute(value, axis, [(source, source + steps) for source in range(first, last)])


def multipole_coefficients(pair_density, expansion):
    moments = jnp.dot(pair_density, expansion, precision=lax.Precision.HIGHEST)
    return jnp.concatenate(
        [
            moments[:, :7],
            moments[:, 7:8] - moments[:, 8:9],
            -moments[:, 7:8] - moments[:, 8:9],
            2.0 * moments[:, 8:9],
        ],
        axis=1,
    )


def axis_factors(anchor, length, corner, centre):
    coord = anchor + jnp.arange(length, dtype=jnp.float32)
    inside = (coord[None, :] >= corner[:, None]) & (coord[None, :] < corner[:, None] + BOX)
    scaled = (coord[None, :] - centre[:, None]) * INV_RC
    bell = jnp.where(inside, jnp.exp(-scaled * scaled), 0.0)
    return (bell, scaled * bell, scaled * scaled * bell)


def compensation_block(anchor, coefficients, centre, corner, valid, shape):
    powers = [axis_factors(anchor[k], shape[k], corner[:, k], centre[:, k]) for k in range(3)]
    weights = coefficients * valid[:, None]
    x_terms = jnp.stack([powers[0][e[0]] for e in EXPONENTS], axis=1) * weights[:, :, None]
    y_terms = jnp.stack([powers[1][e[1]] for e in EXPONENTS], axis=1)
    z_terms = jnp.stack([powers[2][e[2]] for e in EXPONENTS], axis=1)
    count = x_terms.shape[0] * x_terms.shape[1]
    plane = (x_terms[:, :, :, None] * y_terms[:, :, None, :]).reshape(count, shape[0] * shape[1])
    block = lax.dot_general(
        plane,
        z_terms.reshape(count, shape[2]),
        (((0,), (0,)), ((), ())),
        precision=lax.Precision.HIGHEST,
    )
    return block.reshape(shape)


def refine_axis(padded, axis):
    n = padded.shape[axis] - 2
    lower = lax.slice_in_dim(padded, 0, n, axis=axis)
    middle = lax.slice_in_dim(padded, 1, n + 1, axis=axis)
    upper = lax.slice_in_dim(padded, 2, n + 2, axis=axis)
    even = 0.75 * middle + 0.25 * lower
    odd = 0.75 * middle + 0.25 * upper
    shape = list(middle.shape)
    shape[axis] = 2 * n
    return jnp.stack([even, odd], axis=axis + 1).reshape(shape)


def refine(padded):
    for axis in range(3):
        padded = refine_axis(padded, axis)
    return padded


def restrict(field):
    a, b, c = (field.shape[0] // 2, field.shape[1] // 2, field.shape[2] // 2)
    return jnp.sum(field.reshape(a, 2, b, 2, c, 2), axis=(1, 3, 5)) * 0.125


def neighbours(padded):
    total = padded[2:, 1:-1, 1:-1] + padded[:-2, 1:-1, 1:-1]
    total = total + padded[1:-1, 2:, 1:-1] + padded[1:-1, :-2, 1:-1]
    return total + padded[1:-1, 1:-1, 2:] + padded[1:-1, 1:-1, :-2]


def apply_operator(padded, scale):
    return scale * (6.0 * padded[1:-1, 1:-1, 1:-1] - neighbours(padded))


def jacobi(field, source, padded, scale):
    return field + RELAX / (6.0 * scale) * (source - apply_operator(padded, scale))


def widen(field):
    return with_halo(field, (("gx", 0), ("gy", 1), ("gz", 2)), 1)


def faces(field):
    return with_halo(field, (("gx", 0), ("gy", 1), ("gz", 2)), 1)


def per_device(
    coarse_density,
    start_potential,
    pair_density,
    expansion,
    box_corners,
    box_offsets,
    atom_lists,
    atom_counts,
):
    index_x = lax.axis_index("gx")
    index_y = lax.axis_index("gy")
    index_z = lax.axis_index("gz")
    count_y = lax.axis_size("gy")
    count_z = lax.axis_size("gz")
    extent = start_potential.shape
    owned = pair_density.shape[0]
    coefficients = multipole_coefficients(pair_density, expansion)
    corner_own = box_corners.astype(jnp.float32)
    centre_own = corner_own + (BOX - 1) * 0.5 + box_offsets
    packed = jnp.concatenate([coefficients, centre_own, corner_own], axis=1)
    atom_ids = atom_lists[0]
    near = packed[None]
    near = jnp.concatenate([near, shifted(near, "gx", 1)], axis=0)
    near = jnp.concatenate([near, shifted(near, "gy", 1)], axis=0)
    near = jnp.concatenate([near, shifted(near, "gz", 1)], axis=0)
    owner = atom_ids // owned
    local_index = atom_ids % owned
    back_x = index_x - owner // (count_y * count_z)
    back_y = index_y - owner // count_z % count_y
    back_z = index_z - owner % count_z
    slot = jnp.clip((back_z * 4 + back_y * 2 + back_x) * owned + local_index, 0, 8 * owned - 1)
    rows = near.reshape(8 * owned, packed.shape[1])[slot]
    valid = (jnp.arange(atom_ids.shape[0], dtype=jnp.int32) < atom_counts[0]).astype(jnp.float32)
    anchor = (
        (index_x * extent[0]).astype(jnp.float32),
        (index_y * extent[1]).astype(jnp.float32),
        (index_z * extent[2]).astype(jnp.float32),
    )
    compensation = compensation_block(
        anchor, rows[:, :10], rows[:, 10:13], rows[:, 13:16], valid, extent
    )
    total_density = refine(widen(coarse_density)) + compensation

    def vcycle_spread(level, field, source):
        scale = 0.25**level
        if level == LEVELS - 1:
            for sweep in range(COARSE_SWEEPS):
                field = jacobi(field, source, faces(field), scale)
            return field
        field = jacobi(field, source, faces(field), scale)
        rest = source - apply_operator(faces(field), scale)
        coarse_source = restrict(rest)
        correction_rim = widen(
            vcycle_spread(level + 1, jnp.zeros_like(coarse_source), coarse_source)
        )
        field = field + refine(correction_rim)
        field = jacobi(field, source, faces(field), scale)
        return field

    potential = start_potential
    for cycle in range(CYCLES):
        potential = vcycle_spread(0, potential, total_density)
    return (total_density, potential)


def solution(mesh):
    in_specs = (
        P("gx", "gy", "gz"),
        P("gx", "gy", "gz"),
        P(("gx", "gy", "gz"), None),
        P(),
        P(("gx", "gy", "gz"), None),
        P(("gx", "gy", "gz"), None),
        P(("gx", "gy", "gz"), None),
        P(("gx", "gy", "gz")),
    )
    out_specs = (P("gx", "gy", "gz"), P("gx", "gy", "gz"))
    return jax.shard_map(
        per_device, mesh=mesh, in_specs=in_specs, out_specs=out_specs, check_vma=False
    )
```

profile of v0, /device:TPU:228, one launch (start us, length us, event | category | flops | bytes accessed | tf_op | source)
XLA Modules:
  0.0 1037.6 jit_solution(10228284362063514392)
XLA Ops:
  25.5 5.5 collective-permute-start.60
  33.0 5.1 collective-permute-start.33
  132.3 5.4 collective-permute-start.24
  159.9 18.1 %reshape.1902 = f32[8,2,16,2,64,2]{5,4,3,2,1,0:T(8,128)} reshape(f32[16,32,128]{2,1,0:T(8,128)S(1)} %fusion.44) | data formatting | bytes 524288 | tf_op jit(solution)/shard_map/reshape | solution.py:105
  178.1 7.0 reduce_sum.86
  196.3 5.4 collective-permute-start.30
  313.9 5.4 collective-permute-start.72
  338.2 5.4 collective-permute-start.78
  360.3 5.4 collective-permute-start.83
  379.8 5.4 collective-permute-start.87
  434.1 5.4 collective-permute-start.99
  458.8 5.4 collective-permute-start.106
  482.2 5.4 collective-permute-start.111
  519.6 5.4 collective-permute-start.119
  542.2 5.4 collective-permute-start.123
  556.5 5.1 collective-permute-start.126
  585.1 5.4 collective-permute-start.132
  613.9 5.4 collective-permute-start.138
  632.0 18.1 %reshape.1917 = f32[8,2,16,2,64,2]{5,4,3,2,1,0:T(8,128)} reshape(f32[16,32,128]{2,1,0:T(8,128)S(1)} %fusion.15) | data formatting | bytes 524288 | tf_op jit(solution)/shard_map/reshape | solution.py:105
  650.2 7.0 reduce_sum.92
  667.8 5.4 collective-permute-start.144
  694.0 5.4 collective-permute-start.150
  773.0 5.4 collective-permute-start.168
  797.3 5.4 collective-permute-start.174
  819.4 5.4 collective-permute-start.179
  838.9 5.4 collective-permute-start.183
  868.6 5.1 collective-permute-start.190
  891.2 5.4 collective-permute-start.195
  921.3 5.1 collective-permute-start.202
  944.4 5.4 collective-permute-start.207
  981.8 5.4 collective-permute-start.215
  1004.2 5.4 collective-permute-start.219
  (862 shorter events, 830.8 us)
Async XLA Ops:
  1.2 121.2 %collective-permute-start.21 = (f32[1,16,64]{2,1,0:T(8,128)}, f32[1,16,64]{2,1,0:T(8,128)S(1)}, u32[]{:S(2)}, u32[]{:S(2)}) collective-permute-start(f32[1,16,64]{2,1,0:T(8,128)} %broadcast.1576), channel_id=1, source_target_pairs={{64,0},{128,64},{192,128},{256,192},{320,256},{384,320},{448,384},... | collective-permute-start | bytes 12296 | tf_op jit(solution)/shard_map/ppermute | solution.py:36
  3.6 121.9 %collective-permute-start.22 = (f32[1,16,64]{2,1,0:T(8,128)}, f32[1,16,64]{2,1,0:T(8,128)S(1)}, u32[]{:S(2)}, u32[]{:S(2)}) collective-permute-start(f32[1,16,64]{2,1,0:T(8,128)} %broadcast.1576), channel_id=1, source_target_pairs={{0,64},{64,128},{128,192},{192,256},{256,320},{320,384},{384,448},... | collective-permute-start | bytes 12296 | tf_op jit(solution)/shard_map/ppermute | solution.py:33
  7.1 16.4 %collective-permute-start.57 = (f32[1,2,8]{2,1,0:T(2,128)S(1)}, f32[1,2,8]{2,1,0:T(2,128)S(1)}, u32[]{:S(2)}, u32[]{:S(2)}) collective-permute-start(f32[1,2,8]{2,1,0:T(2,128)S(1)} %broadcast.1590), channel_id=1, source_target_pairs={{64,0},{128,64},{192,128},{256,192},{320,256},{384,320},{448,384},... | collective-permute-start | bytes 200 | tf_op jit(solution)/shard_map/ppermute | solution.py:36
  10.7 12.9 %collective-permute-start.58 = (f32[1,2,8]{2,1,0:T(2,128)S(1)}, f32[1,2,8]{2,1,0:T(2,128)S(1)}, u32[]{:S(2)}, u32[]{:S(2)}) collective-permute-start(f32[1,2,8]{2,1,0:T(2,128)S(1)} %broadcast.1590), channel_id=1, source_target_pairs={{0,64},{64,128},{128,192},{192,256},{256,320},{320,384},{384,448},... | collective-permute-start | bytes 200 | tf_op jit(solution)/shard_map/ppermute | solution.py:33
  13.0 25.2 %collective-permute-start.45 = (f32[1,4,16]{2,1,0:T(4,128)S(1)}, f32[1,4,16]{2,1,0:T(4,128)S(1)}, u32[]{:S(2)}, u32[]{:S(2)}) collective-permute-start(f32[1,4,16]{2,1,0:T(4,128)S(1)} %broadcast.1586), channel_id=1, source_target_pairs={{64,0},{128,64},{192,128},{256,192},{320,256},{384,320},{448,384},... | collective-permute-start | bytes 776 | tf_op jit(solution)/shard_map/ppermute | solution.py:36
  31.0 9.1 collective-permute-start.46
  33.0 9.7 collective-permute-start.33
  40.1 10.3 collective-permute-start.6
  42.8 15.1 %collective-permute-start = (f32[1,16,64]{2,1,0:T(8,128)S(1)}, f32[1,16,64]{2,1,0:T(8,128)S(1)}, u32[]{:S(2)}, u32[]{:S(2)}) collective-permute-start(f32[1,16,64]{2,1,0:T(8,128)S(1)} %get-tuple-element.124), channel_id=1, source_target_pairs={{0,64},{64,128},{128,192},{192,256},{256,320},{320,384},{384,448},... | collective-permute-start | bytes 12296 | tf_op jit(solution)/shard_map/ppermute | solution.py:33
  44.9 19.0 %collective-permute-start.1 = (f32[1,16,64]{2,1,0:T(8,128)S(1)}, f32[1,16,64]{2,1,0:T(8,128)S(1)}, u32[]{:S(2)}, u32[]{:S(2)}) collective-permute-start(f32[1,16,64]{2,1,0:T(8,128)S(1)} %get-tuple-element.123), channel_id=1, source_target_pairs={{64,0},{128,64},{192,128},{256,192},{320,256},{384,320},{448,384},... | collective-permute-start | bytes 12296 | tf_op jit(solution)/shard_map/ppermute | solution.py:36
  55.9 40.7 %collective-permute-start.10 = (f32[1,32,128]{2,1,0:T(8,128)S(1)}, f32[1,32,128]{2,1,0:T(8,128)S(1)}, u32[]{:S(2)}, u32[]{:S(2)}) collective-permute-start(f32[1,32,128]{2,1,0:T(8,128)S(1)} %get-tuple-element.60), channel_id=1, source_target_pairs={{0,64},{64,128},{128,192},{192,256},{256,320},{320,384},{384,448},... | collective-permute-start | bytes 49160 | tf_op jit(solution)/shard_map/ppermute | solution.py:33
  73.0 15.6 %collective-permute-start.4 = (f32[10,18,1]{2,1,0:T(8,128)S(1)}, f32[10,18,1]{2,1,0:T(8,128)S(1)}, u32[]{:S(2)}, u32[]{:S(2)}) collective-permute-start(f32[10,18,1]{2,1,0:T(8,128)S(1)} %get-tuple-element.89), channel_id=1, source_target_pairs={{0,1},{1,2},{2,3},{3,4},{4,5},{5,6},{6,7},{8,9},{9,10},{10,11},{11... | collective-permute-start | bytes 2168 | tf_op jit(solution)/shard_map/ppermute | solution.py:33
  75.1 18.6 %collective-permute-start.5 = (f32[10,18,1]{2,1,0:T(8,128)S(1)}, f32[10,18,1]{2,1,0:T(8,128)S(1)}, u32[]{:S(2)}, u32[]{:S(2)}) collective-permute-start(f32[10,18,1]{2,1,0:T(8,128)S(1)} %get-tuple-element.90), channel_id=1, source_target_pairs={{1,0},{2,1},{3,2},{4,3},{5,4},{6,5},{7,6},{9,8},{10,9},{11,10},{12... | collective-permute-start | bytes 2168 | tf_op jit(solution)/shard_map/ppermute | solution.py:36
  93.7 131.0 %collective-permute-start.48 = (f32[4,1,16]{2,1,0:T(1,128)}, f32[4,1,16]{2,1,0:T(1,128)S(1)}, u32[]{:S(2)}, u32[]{:S(2)}) collective-permute-start(f32[4,1,16]{2,1,0:T(1,128)} %get-tuple-element.231), channel_id=1, source_target_pairs={{0,8},{8,16},{16,24},{24,32},{32,40},{40,48},{48,56},{1,9},{9,17},... | collective-permute-start | bytes 776 | tf_op jit(solution)/shard_map/ppermute | solution.py:33
  108.6 9.1 collective-permute-start.14
  114.0 110.8 %collective-permute-start.47 = (f32[4,1,16]{2,1,0:T(1,128)}, f32[4,1,16]{2,1,0:T(1,128)}, u32[]{:S(2)}, u32[]{:S(2)}) collective-permute-start(f32[4,1,16]{2,1,0:T(1,128)} %get-tuple-element.232), channel_id=1, source_target_pairs={{8,0},{16,8},{24,16},{32,24},{40,32},{48,40},{56,48},{9,1},{17,9},... | collective-permute-start | bytes 776 | tf_op jit(solution)/shard_map/ppermute | solution.py:36
  117.8 73.4 %collective-permute-start.35 = (f32[6,1,32]{2,1,0:T(1,128)}, f32[6,1,32]{2,1,0:T(1,128)}, u32[]{:S(2)}, u32[]{:S(2)}) collective-permute-start(f32[6,1,32]{2,1,0:T(1,128)} %get-tuple-element.169), channel_id=1, source_target_pairs={{8,0},{16,8},{24,16},{32,24},{40,32},{48,40},{56,48},{9,1},{17,9},... | collective-permute-start | bytes 2312 | tf_op jit(solution)/shard_map/ppermute | solution.py:36
  128.4 9.4 collective-permute-start.23
  148.4 9.1 collective-permute-start.20
  153.4 31.7 %collective-permute-start.25 = (f32[10,18,1]{2,1,0:T(8,128)S(1)}, f32[10,18,1]{2,1,0:T(8,128)S(1)}, u32[]{:S(2)}, u32[]{:S(2)}) collective-permute-start(f32[10,18,1]{2,1,0:T(8,128)S(1)} %get-tuple-element.85), channel_id=1, source_target_pairs={{1,0},{2,1},{3,2},{4,3},{5,4},{6,5},{7,6},{9,8},{10,9},{11,10},{12... | collective-permute-start | bytes 2168 | tf_op jit(solution)/shard_map/ppermute | solution.py:36
  157.5 27.6 %collective-permute-start.26 = (f32[10,18,1]{2,1,0:T(8,128)S(1)}, f32[10,18,1]{2,1,0:T(8,128)S(1)}, u32[]{:S(2)}, u32[]{:S(2)}) collective-permute-start(f32[10,18,1]{2,1,0:T(8,128)S(1)} %get-tuple-element.86), channel_id=1, source_target_pairs={{0,1},{1,2},{2,3},{3,4},{4,5},{5,6},{6,7},{8,9},{9,10},{10,11},{11... | collective-permute-start | bytes 2168 | tf_op jit(solution)/shard_map/ppermute | solution.py:33
  194.3 9.3 collective-permute-start.29
  196.3 9.8 collective-permute-start.30
  227.5 10.3 collective-permute-start.42
  231.5 15.5 %collective-permute-start.49 = (f32[4,6,1]{2,0,1:T(4,128)S(1)}, f32[4,6,1]{2,0,1:T(4,128)S(1)}, u32[]{:S(2)}, u32[]{:S(2)}) collective-permute-start(f32[4,6,1]{2,0,1:T(4,128)S(1)} %get-tuple-element.217), channel_id=1, source_target_pairs={{1,0},{2,1},{3,2},{4,3},{5,4},{6,5},{7,6},{9,8},{10,9},{11,10},{12... | collective-permute-start | bytes 296 | tf_op jit(solution)/shard_map/ppermute | solution.py:36
  233.5 13.5 %collective-permute-start.50 = (f32[4,6,1]{2,0,1:T(4,128)S(1)}, f32[4,6,1]{2,0,1:T(4,128)S(1)}, u32[]{:S(2)}, u32[]{:S(2)}) collective-permute-start(f32[4,6,1]{2,0,1:T(4,128)S(1)} %get-tuple-element.218), channel_id=1, source_target_pairs={{0,1},{1,2},{2,3},{3,4},{4,5},{5,6},{6,7},{8,9},{9,10},{10,11},{11... | collective-permute-start | bytes 296 | tf_op jit(solution)/shard_map/ppermute | solution.py:33
  259.7 10.2 collective-permute-start.54
  265.6 12.9 %collective-permute-start.61 = (f32[3,4,1]{2,1,0:T(4,128)S(1)}, f32[3,4,1]{2,1,0:T(4,128)S(1)}, u32[]{:S(2)}, u32[]{:S(2)}) collective-permute-start(f32[3,4,1]{2,1,0:T(4,128)S(1)} %get-tuple-element.256), channel_id=1, source_target_pairs={{1,0},{2,1},{3,2},{4,3},{5,4},{6,5},{7,6},{9,8},{10,9},{11,10},{12... | collective-permute-start | bytes 152 | tf_op jit(solution)/shard_map/ppermute | solution.py:36
  267.5 11.0 %collective-permute-start.62 = (f32[3,4,1]{2,1,0:T(4,128)S(1)}, f32[3,4,1]{2,1,0:T(4,128)S(1)}, u32[]{:S(2)}, u32[]{:S(2)}) collective-permute-start(f32[3,4,1]{2,1,0:T(4,128)S(1)} %get-tuple-element.257), channel_id=1, source_target_pairs={{0,1},{1,2},{2,3},{3,4},{4,5},{5,6},{6,7},{8,9},{9,10},{10,11},{11... | collective-permute-start | bytes 152 | tf_op jit(solution)/shard_map/ppermute | solution.py:33
  565.2 8.8 collective-permute-start.128
  594.0 8.8 collective-permute-start.134
  622.9 8.8 collective-permute-start.140
  (212 other events, 2581.4 us)
where the time goes:
time: 1050 us; the launch traced here: 1040 us
  starting transfers between devices  674 us (64%)
  waiting for transfers between devices  259 us (25%)
  local copies, waits for them, and re-layouts  62.4 us (6%)
  other arithmetic  33.3 us (3%)
    ppermute x111, starting transfers between devices, with_halo(): lax.ppermute(lax.slice_in_dim(block, block.shape[dim] - width, None, axis...  337 us
    ppermute x111, starting transfers between devices, with_halo(): lax.ppermute(lax.slice_in_dim(block, 0, width, axis=dim), axis, backward)  328 us
    ppermute x111, waiting for transfers between devices, with_halo(): lax.ppermute(lax.slice_in_dim(block, block.shape[dim] - width, None, axis...  166 us
    ppermute x111, waiting for transfers between devices, with_halo(): lax.ppermute(lax.slice_in_dim(block, 0, width, axis=dim), axis, backward)  93 us
    reshape x6, local copies, waits for them, and re-layouts, restrict(): return jnp.sum(field.reshape(a, 2, b, 2, c, 2), axis=(1, 3, 5)) * 0.125  40.9 us
  transfers between devices with their start and end apart: 225, of which 104 were waited for; matrix products, arithmetic and copies ran while one was open for 5% of the time, Pallas kernels for 0%

commit v1 on v0

v1 whole, which is shorter than its diff:
```python
import itertools

import jax
import jax.numpy as jnp
from jax import lax
from jax.experimental import pallas as pl
from jax.experimental.pallas import tpu as pltpu
from jax.sharding import PartitionSpec as P

F32 = jnp.float32
BF16 = jnp.bfloat16
MESH = pl.DeviceIdType.MESH
ALPHA = 0.8 / 6.0
AXES = ("gx", "gy", "gz")
DIRS = [d for d in itertools.product((-1, 0, 1), repeat=3) if d != (0, 0, 0)]
DIRS.sort(key=lambda d: sum(map(abs, d)))
UP7 = [d for d in itertools.product((0, 1), repeat=3) if d != (0, 0, 0)]
RING = list(range(1, 8))
PHASE2 = [(k, dz) for k in range(8) for dz in (-1, 0, 1) if (k, dz) != (0, 0)]
N_ATOM, N_DIR, N_RING, N_P2 = len(UP7), len(DIRS), len(RING), len(PHASE2)
SEM_V = N_ATOM
SEM_RHO = SEM_V + N_DIR
SEM_F = SEM_RHO + N_DIR
SEM_CYCLE = SEM_F + N_DIR
PER_CYCLE = 2 * N_DIR + N_RING + N_P2
N_SEMS = SEM_CYCLE + 2 * PER_CYCLE


def iota(shape, dim):
    return lax.broadcasted_iota(jnp.int32, shape, dim)


def wrapped(lane, cut, lanes):
    return jnp.where(lane < cut, lane, lane - lanes)


def split(a):
    hi = a.astype(BF16)
    return hi, (a - hi.astype(F32)).astype(BF16)


def dot(a, b):
    return jnp.dot(a, b, preferred_element_type=F32)


def mm(a, m):
    hi, lo = split(a)
    return dot(hi, m) + dot(lo, m)


def restrict_matrix(rows, rcut, cols, ccut):
    fine = wrapped(iota((rows, cols), 0), rcut, rows)
    coarse = wrapped(iota((rows, cols), 1), ccut, cols)
    return jnp.where((fine >> 1) == coarse, 1.0, 0.0).astype(BF16)


def prolong_matrix(rows, rcut, cols, ccut):
    coarse = wrapped(iota((rows, cols), 0), rcut, rows)
    fine = wrapped(iota((rows, cols), 1), ccut, cols)
    centre = fine >> 1
    other = jnp.where((fine & 1) == 0, centre - 1, centre + 1)
    return jnp.where(coarse == centre, 0.75, jnp.where(coarse == other, 0.25, 0.0)).astype(BF16)


def grid_mask(shape, starts, sizes, cut, window):
    x = iota(shape, 0) + starts[0]
    y = iota(shape, 1) + starts[1]
    z = wrapped(iota(shape, 2), cut, shape[2])
    near = (z >= window[0]) & (z < window[1])
    z = z + starts[2]
    inside = (x >= 0) & (x < sizes[0]) & (y >= 0) & (y < sizes[1]) & (z >= 0) & (z < sizes[2])
    return jnp.where(inside & near, 1.0, 0.0)


def neighbours(ref, first, count):
    c = ref[pl.ds(first, count)]
    rows, lanes = c.shape[1], c.shape[2]
    total = ref[pl.ds(first - 1, count)] + ref[pl.ds(first + 1, count)]
    total = total + pltpu.roll(c, 1, 1) + pltpu.roll(c, rows - 1, 1)
    return c, total + pltpu.roll(c, 1, 2) + pltpu.roll(c, lanes - 1, 2)


def expand_rows(es, ye, yo, r0, nr):
    def rows(start):
        return es[:, pl.ds(start, nr), :]

    mid = 0.75 * rows(r0)
    ye[...] = mid + 0.25 * rows(r0 - 1)
    yo[...] = mid + 0.25 * rows(r0 + 1)


def store_pairs(out, index, even, odd):
    n = even.shape[0]
    for h in range(even.shape[1] // 128):
        s = slice(128 * h, 128 * h + 128)
        half = out.at[h] if even.shape[1] > 128 else out
        half[index, pl.ds(0, n, 2), :] = even[:, s]
        half[index, pl.ds(1, n, 2), :] = odd[:, s]


def expand_planes(ye, yo, out, f0, c0, k):
    e, o = 0.75 * ye[k + c0], 0.75 * yo[k + c0]
    store_pairs(out, f0 + 2 * k, e + 0.25 * ye[k + c0 - 1], o + 0.25 * yo[k + c0 - 1])
    store_pairs(out, f0 + 2 * k + 1, e + 0.25 * ye[k + c0 + 1], o + 0.25 * yo[k + c0 + 1])


def halve_rows(ref, start, count):
    return ref[pl.ds(start, count, 2), :] + ref[pl.ds(start + 1, count, 2), :]


def kernel(
    rho, v0, pair, expn, corner, offset, dens, pot,
    vf, v1, ff, wf, zl0, zh0, zs0,
    f1, zl1, zh1, zs1, g1, a0, s0, es0, ye0, yo0, e1, w1, es1, ye1, yo1,
    t2, f2, e2, w2, s1, es2, ye2, yo2,
    x1, xs, y1, f3, e3, w3, s2, ts, es3, ye3, yo3,
    f4, v4, a3, s3,
    at, pln, k0, k1, k2, k3, k4, ss, rs,
):
    gx, gy, gz = (lax.axis_index(a) for a in AXES)
    here = (gx, gy, gz)

    def peer(d):
        return tuple(i if s == 0 else lax.rem(i + (s + 8), 8) for i, s in zip(here, d))

    barrier = pltpu.get_barrier_semaphore()
    reached = []
    for d in DIRS + [(k, 0, 0) for k in RING] + [(0, k, dz) for k, dz in PHASE2]:
        d = tuple(s % 8 for s in d)
        if d not in reached:
            reached.append(d)
    for d in reached:
        pl.semaphore_signal(barrier, inc=1, device_id=peer(d), device_id_type=MESH)

    for ref in (v1.at[0], v1.at[27], g1, f3, e3, f4, v4):
        ref[...] = jnp.zeros(ref.shape, F32)
    k0[...] = grid_mask((28, 48, 256), (16 * gx - 6, 32 * gy - 8, 128 * gz), (128, 256, 1024), 192, (-8, 136))
    k1[...] = grid_mask((16, 32, 128), (8 * gx - 4, 16 * gy - 8, 64 * gz), (64, 128, 512), 96, (-8, 72))
    k2[...] = grid_mask((12, 24, 128), (4 * gx - 4, 8 * gy - 8, 32 * gz), (32, 64, 256), 80, (-24, 56))
    k3[...] = grid_mask((16, 48, 128), (0, -8, 16 * gz), (16, 32, 128), 64, (-24, 40))
    k4[...] = grid_mask((8, 32, 128), (0, -8, 8 * gz), (8, 16, 64), 64, (-16, 24))

    vf[6:22, 8:40, 0:128] = v0[...]
    f1[0, 4:12, 8:24, 0:64] = rho[...]

    hi_prec = lax.Precision.HIGHEST
    m = iota((9, 128), 0)
    c = iota((9, 128), 1)
    one = jnp.where((c < 7) & (m == c), 1.0, 0.0)
    one = one + jnp.where((c == 7) & (m == 7), 1.0, 0.0) - jnp.where((c == 7) & (m == 8), 1.0, 0.0)
    one = one - jnp.where((c == 8) & (m >= 7), 1.0, 0.0) + jnp.where((c == 9) & (m == 8), 2.0, 0.0)
    moments = jnp.dot(pair[...], expn[...], precision=hi_prec)
    packed = jnp.dot(moments, one, precision=hi_prec)
    corners = corner[...].astype(F32)
    centres = corners + 5.5 + offset[...]
    p3 = iota((3, 128), 0)
    l3 = iota((3, 128), 1)
    packed = packed + jnp.dot(centres, jnp.where(l3 == p3 + 10, 1.0, 0.0), precision=hi_prec)
    packed = packed + jnp.dot(corners, jnp.where(l3 == p3 + 13, 1.0, 0.0), precision=hi_prec)
    at[0:16, :] = packed

    pl.semaphore_wait(barrier, len(reached))

    def rcopy(src, dst, k, d):
        return pltpu.make_async_remote_copy(
            src_ref=src, dst_ref=dst, send_sem=ss.at[k], recv_sem=rs.at[k], device_id=peer(d), device_id_type=MESH
        )

    def atom_copies():
        return [
            rcopy(at.at[0:16], at.at[16 * k + 16 : 16 * k + 32], k, d) for k, d in enumerate(UP7)
        ]

    def frame_slices(d, nx, hx, ny):
        src, dst = [], []
        for s, n, h, o in ((d[0], nx, hx, hx), (d[1], ny, 8, 8)):
            if s == 0:
                src.append(slice(o, o + n))
                dst.append(slice(o, o + n))
            elif s > 0:
                src.append(slice(o + n - h, o + n))
                dst.append(slice(0, h))
            else:
                src.append(slice(o, o + h))
                dst.append(slice(o + n, o + n + h))
        return tuple(src), tuple(dst)

    def copies0(frame, q, base):
        out = []
        for k, d in enumerate(DIRS):
            src, dst = frame_slices(d, 16, 6, 32)
            if d[2] == 0:
                out.append(rcopy(frame.at[src + (slice(0, 128),)], frame.at[dst + (slice(0, 128),)], base + k, d))
            else:
                rows = slice(src[1].start - 8, src[1].stop - 8)
                zr = zh0 if d[2] > 0 else zl0
                out.append(rcopy(zs0.at[q, 1 if d[2] > 0 else 0, rows], zr.at[q, 1 - d[0], dst[1]], base + k, d))
        return out

    def copies1(q, base):
        out = []
        for k, d in enumerate(DIRS):
            src, dst = frame_slices(d, 8, 4, 16)
            if d[2] == 0:
                out.append(rcopy(f1.at[(q,) + src], f1.at[(q,) + dst], base + k, d))
            else:
                rows = slice(src[1].start - 8, src[1].stop - 8)
                zr = zh1 if d[2] > 0 else zl1
                out.append(rcopy(zs1.at[q, rows], zr.at[q, 1 - d[0], dst[1]], base + k, d))
        return out

    def copies2(q, base):
        mine = t2.at[q, 1, 1, 8:16]
        return [
            rcopy(mine, t2.at[q, 1 - d[2], 1 - d[0], 8 * (1 - d[1]) : 8 * (1 - d[1]) + 8], base + k, d)
            for k, d in enumerate(DIRS)
        ]

    def copies3a(q, base):
        return [rcopy(x1.at[q, 0], x1.at[q, n], base + k, (n, 0, 0)) for k, n in enumerate(RING)]

    def copies3b(q, base):
        return [
            rcopy(y1.at[q, 1, gy], y1.at[q, 1 - dz, gy], base + k, (0, n, dz)) for k, (n, dz) in enumerate(PHASE2)
        ]

    def start(copies):
        for item in copies:
            item.start()

    def wait_recv(copies):
        for item in copies:
            item.wait_recv()

    def wait_send(copies):
        for item in copies:
            item.wait_send()

    def pack0(frame, q):
        lane = iota((32, 128), 1)
        lo = hi = jnp.zeros((32, 128), F32)
        for x in range(16):
            t = frame[6 + x, 8:40, 0:128]
            if x:
                t = pltpu.roll(t, 8 * x, 1)
            h = (8 * x - 8) % 128
            lo = jnp.where((lane >= 8 * x) & (lane < 8 * x + 8), t, lo)
            hi = jnp.where((lane >= h) & (lane < h + 8), t, hi)
        zs0[q, 0] = lo
        zs0[q, 1] = hi

    def unpack0(frame, q):
        lane = iota((48, 128), 1)

        def body(i, carry):
            slot = jnp.where(i < 6, 0, jnp.where(i < 22, 1, 2))
            sx = jnp.where(i < 6, i + 10, jnp.where(i < 22, i - 6, i - 22))
            t = jnp.where((lane >= 8 * sx) & (lane < 8 * sx + 8), zl0[q, slot], zh0[q, slot])
            t = pltpu.roll(t, lax.rem(128 - 8 * sx, 128), 1)
            frame[i, :, 0:128] = frame[i, :, 0:128] * k0[i, :, 0:128]
            frame[i, :, 128:256] = jnp.where((lane < 8) | (lane >= 120), t, 0.0) * k0[i, :, 128:256]
            return carry

        lax.fori_loop(0, 28, body, 0)

    def pack1(q):
        lane = iota((16, 128), 1)
        out = jnp.zeros((16, 128), F32)
        for x in range(8):
            t = f1[q, 4 + x, 8:24, :]
            lo = t if x == 0 else pltpu.roll(t, 16 * x, 1)
            hi = t if x == 3 else pltpu.roll(t, (16 * x - 48) % 128, 1)
            out = jnp.where((lane >= 16 * x) & (lane < 16 * x + 8), lo, out)
            out = jnp.where((lane >= 16 * x + 8) & (lane < 16 * x + 16), hi, out)
        zs1[q] = out

    def unpack1(q):
        lane = iota((32, 128), 1)
        for i in range(16):
            slot = 0 if i < 4 else 1 if i < 12 else 2
            sx = (4 + i) % 8 if i < 4 else (i - 4) % 8
            lo = zl1[q, slot]
            hi = zh1[q, slot]
            if (64 - 16 * sx) % 128:
                lo = pltpu.roll(lo, (64 - 16 * sx) % 128, 1)
            if (112 - 16 * sx) % 128:
                hi = pltpu.roll(hi, (112 - 16 * sx) % 128, 1)
            t = jnp.where(lane < 64, f1[q, i], jnp.where(lane < 72, lo, jnp.where(lane >= 120, hi, 0.0)))
            f1[q, i] = t * k1[i]

    def unpack2(q):
        lane = iota((24, 128), 1)
        for i in range(12):
            slot, sx = i // 4, i % 4
            below, mid, above = t2[q, 0, slot], t2[q, 1, slot], t2[q, 2, slot]
            if sx:
                mid = pltpu.roll(mid, 128 - 32 * sx, 1)
            if sx != 1:
                above = pltpu.roll(above, (32 - 32 * sx) % 128, 1)
            if sx != 3:
                below = pltpu.roll(below, 96 - 32 * sx, 1)
            t = jnp.where(lane < 32, mid, jnp.where(lane < 64, above, jnp.where(lane >= 96, below, 0.0)))
            f2[i] = t * k2[i]

    def unpack3(q):
        lane = iota((64, 128), 1)
        keep = k3[0, 8:9, :]

        def body(g, carry):
            def turned(slot, target):
                return pltpu.roll(y1[q, slot].reshape(64, 128), lax.rem(128 + target - 16 * g, 128), 1)

            t = jnp.where(lane < 16, turned(1, 0), 0.0)
            t = jnp.where((lane >= 16) & (lane < 32), turned(2, 16), t)
            t = jnp.where(lane >= 112, turned(0, 112), t) * keep
            for h in range(8):
                for xl in range(2):
                    f3[4 + 2 * g + xl, 8 + 4 * h : 12 + 4 * h, :] = t[8 * h + 4 * xl : 8 * h + 4 * xl + 4]
            return carry

        lax.fori_loop(0, 8, body, 0)

    def prolong0(source):
        es0[...] = mm(source.reshape(512, 128), prolong_matrix(128, 96, 256, 192)).reshape(16, 32, 256)

        def rows(i, carry):
            mid = 0.75 * es0[i, 4:28, :]
            ye0[i] = mid + 0.25 * es0[i, 3:27, :]
            yo0[i] = mid + 0.25 * es0[i, 5:29, :]
            return carry

        lax.fori_loop(0, 16, rows, 0)

        def planes(k, carry):
            expand_planes(ye0, yo0, wf, 0, 1, k)
            return carry

        lax.fori_loop(0, 14, planes, 0)

    atoms = atom_copies()
    start(atoms)
    pack1(0)
    rho_copies = copies1(0, SEM_RHO)
    start(rho_copies)
    pack0(vf, 0)
    v_copies = copies0(vf, 0, SEM_V)
    start(v_copies)

    wait_recv(rho_copies)
    wait_send(rho_copies)
    unpack1(0)
    prolong0(f1[0])

    wait_recv(atoms)
    by_atom = at[...]
    by_param = by_atom.T

    def factor(coord, centre, low):
        u = (coord - centre) * 0.5
        e = jnp.where((coord >= low) & (coord < low + 12.0), jnp.exp(-u * u), 0.0)
        return u, e

    def row(k):
        return by_param[k : k + 1, :]

    def coordinates(shape, dim, first):
        return (iota(shape, dim) + first).astype(F32)

    ux, ex = factor(coordinates((16, 128), 0, 16 * gx), row(10), row(13))
    uy, ey = factor(coordinates((32, 128), 0, 32 * gy), row(11), row(14))
    uz, ez = factor(coordinates((128, 128), 1, 128 * gz), by_atom[:, 12:13], by_atom[:, 15:16])
    uex = ux * ex
    p00 = row(0) * ex + row(1) * uex + row(7) * (ux * uex)
    p01 = row(2) * ex + row(4) * uex
    p02 = row(8) * ex
    p10 = row(3) * ex + row(6) * uex
    p11 = row(5) * ex
    p20 = row(9) * ex
    uey = uy * ey
    uuey = uy * uey
    for x in range(16):
        s = slice(x, x + 1)
        pln[32 * x : 32 * x + 32, 0:128] = p00[s] * ey + p01[s] * uey + p02[s] * uuey
        pln[32 * x : 32 * x + 32, 128:256] = p10[s] * ey + p11[s] * uey
        pln[32 * x : 32 * x + 32, 256:384] = p20[s] * ey
    uez = uz * ez
    z_hi, z_lo = split(jnp.concatenate([ez, uez, uz * uez], axis=0))
    p_hi, p_lo = split(pln[...])
    block = dot(p_hi, z_hi) + dot(p_hi, z_lo) + dot(p_lo, z_hi)
    block = block.reshape(16, 32, 128) + wf[0, 6:22, 8:40, :]
    dens[...] = block
    ff[6:22, 8:40, 0:128] = block

    pack0(ff, 1)
    f_copies = copies0(ff, 1, SEM_F)
    start(f_copies)
    wait_recv(v_copies)
    wait_send(v_copies)
    unpack0(vf, 0)
    wait_recv(f_copies)
    wait_send(f_copies)
    unpack0(ff, 1)

    def cycle(q, carry):
        base = SEM_CYCLE + q * PER_CYCLE
        c1 = copies1(q + 1, base)
        c2 = copies2(q, base + N_DIR)
        c3a = copies3a(q, base + 2 * N_DIR)
        c3b = copies3b(q, base + 2 * N_DIR + N_RING)

        def pre(i, carry):
            c, nb = neighbours(vf, 2 * i + 1, 2)
            s = pl.ds(2 * i + 1, 2)
            v1[s] = (0.2 * c + ALPHA * (ff[s] + nb)) * k0[s]
            return carry

        lax.fori_loop(0, 13, pre, 0)

        def residual(k, carry):
            c, nb = neighbours(v1, 4 + 2 * k, 2)
            r = ff[pl.ds(4 + 2 * k, 2)] - 6.0 * c + nb
            r = r[0] + r[1]
            s0[0] = r[:, 0:128]
            s0[1] = r[:, 128:256]
            a0[k] = jnp.concatenate([halve_rows(s0.at[h], 0, 24) for h in range(2)], axis=1)
            return carry

        lax.fori_loop(0, 10, residual, 0)
        g = 0.125 * mm(a0[...].reshape(240, 256), restrict_matrix(256, 192, 128, 96))
        g1[:, 4:28, :] = g.reshape(10, 24, 128)
        g1[...] = g1[...] * k1[3:13]
        f1[q + 1, 4:12, 8:24, :] = g1[1:9, 8:24, :]

        c, nb = neighbours(g1, 1, 8)
        r = (0.2 * c + ALPHA * nb).reshape(4, 2, 32, 128)
        s1[...] = r[:, 0] + r[:, 1]
        parts = jnp.concatenate(
            [s1[x, pl.ds(8, 8, 2), :] + s1[x, pl.ds(9, 8, 2), :] for x in range(4)], axis=1
        )
        row_at = iota((512, 128), 0)
        col_at = iota((512, 128), 1)
        lane_at = row_at & 127
        m2 = jnp.where((lane_at < 64) & ((row_at >> 7) * 32 + (lane_at >> 1) == col_at), 1.0, 0.0).astype(BF16)
        t2[q, 1, 1, 8:16] = 0.125 * mm(parts, m2)
        start(c2)
        pack1(q + 1)
        start(c1)

        wait_recv(c2)
        unpack2(q)
        c, nb = neighbours(f2, 4, 4)
        r = (0.2 * c + ALPHA * nb).reshape(2, 2, 24, 128)
        r = r[:, 0] + r[:, 1]
        s2[0:8] = r[0, 8:16]
        s2[8:16] = r[1, 8:16]
        row_at = iota((128, 128), 0)
        col_at = iota((128, 128), 1)
        m3 = jnp.where((row_at < 32) & (16 * gx + (row_at >> 1) == col_at), 1.0, 0.0).astype(BF16)
        x1[q, 0] = 0.125 * mm(halve_rows(s2, 0, 8), m3)
        start(c3a)
        wait_recv(c3a)
        total = x1[q, 0]
        for n in RING:
            total = total + x1[q, n]
        y1[q, 1, gy] = total
        start(c3b)
        wait_recv(c3b)
        unpack3(q)

        c, nb = neighbours(f3, 4, 16)
        r = (0.2 * c + ALPHA * nb).reshape(8, 2, 48, 128)
        s3[...] = r[:, 0] + r[:, 1]
        a3[...] = s3[:, pl.ds(8, 16, 2), :] + s3[:, pl.ds(9, 16, 2), :]
        g = 0.125 * mm(a3[...].reshape(128, 128), restrict_matrix(128, 64, 128, 64))
        f4[1:9, 8:24, :] = g.reshape(8, 16, 128) * k4[:, 8:24, :]

        weight4, weight3, weight2, weight1 = (ALPHA * 4.0**level for level in (4, 3, 2, 1))
        v4[1:9] = weight4 * f4[1:9]
        for _ in range(3):
            c, nb = neighbours(v4, 1, 8)
            v4[1:9] = (0.2 * c + ALPHA * nb + weight4 * f4[1:9]) * k4[...]

        es3[...] = mm(v4[...].reshape(320, 128), prolong_matrix(128, 64, 128, 64)).reshape(10, 32, 128)
        expand_rows(es3, ye3, yo3, 4, 24)
        for k in range(8):
            expand_planes(ye3, yo3, w3, 4, 1, k)
        rhs = weight3 * f3[4:20]
        e3[4:20] = (rhs + w3[4:20]) * k3[...]
        c, nb = neighbours(e3, 4, 16)
        e3[4:20] = (0.2 * c + ALPHA * nb + rhs) * k3[...]

        near = e3[pl.ds(2 * gx + 1, 8)].reshape(384, 128)
        es2[...] = mm(near, prolong_matrix(128, 64, 128, 80)).reshape(8, 48, 128)
        expand_rows(es2, ye2, yo2, 4 * gy + 4, 12)
        for k in range(6):
            expand_planes(ye2, yo2, w2, 0, 1, k)
        rhs = weight2 * f2[...]
        e2[...] = (rhs + w2[...]) * k2[...]
        c, nb = neighbours(e2, 1, 10)
        e2[1:11] = (0.2 * c + ALPHA * nb + rhs[1:11]) * k2[1:11]

        es1[...] = mm(e2[...].reshape(288, 128), prolong_matrix(128, 80, 128, 96)).reshape(12, 24, 128)
        expand_rows(es1, ye1, yo1, 4, 16)
        for k in range(8):
            expand_planes(ye1, yo1, w1, 0, 2, k)
        wait_recv(c1)
        wait_send(c1)
        unpack1(q + 1)
        rhs = weight1 * f1[q + 1]
        e1[...] = (rhs + w1[...]) * k1[...]
        c, nb = neighbours(e1, 1, 14)
        e1[1:15] = (0.2 * c + ALPHA * nb + rhs[1:15]) * k1[1:15]

        prolong0(e1[...])

        def correct(i, carry):
            s = pl.ds(2 * i, 2)
            for h in range(2):
                z = slice(128 * h, 128 * h + 128)
                v1[s, :, z] = (v1[s, :, z] + wf[h, s]) * k0[s, :, z]
            return carry

        lax.fori_loop(0, 14, correct, 0)

        def post(i, carry):
            c, nb = neighbours(v1, 2 * i + 1, 2)
            s = pl.ds(2 * i + 1, 2)
            vf[s] = (0.2 * c + ALPHA * (ff[s] + nb)) * k0[s]
            return carry

        lax.fori_loop(0, 13, post, 0)
        wait_send(c2)
        wait_send(c3a)
        wait_send(c3b)
        return carry

    lax.fori_loop(0, 2, cycle, 0)
    pot[...] = vf[6:22, 8:40, 0:128]
    wait_send(atoms)


def scratch():
    def vm(*shape):
        return pltpu.VMEM(shape, F32)

    return [
        vm(28, 48, 256), vm(28, 48, 256), vm(28, 48, 256), vm(2, 28, 48, 128),
        vm(2, 3, 48, 128), vm(2, 3, 48, 128), vm(2, 2, 32, 128),
        vm(3, 16, 32, 128), vm(3, 3, 32, 128), vm(3, 3, 32, 128), vm(3, 16, 128),
        vm(10, 32, 128), vm(10, 24, 256), vm(2, 48, 128), vm(16, 32, 256), vm(16, 24, 256), vm(16, 24, 256),
        vm(16, 32, 128), vm(16, 32, 128), vm(12, 24, 128), vm(12, 16, 128), vm(12, 16, 128),
        vm(2, 3, 3, 24, 128), vm(12, 24, 128), vm(12, 24, 128), vm(12, 24, 128), vm(4, 32, 128),
        vm(8, 48, 128), vm(8, 12, 128), vm(8, 12, 128),
        vm(2, 8, 8, 128), vm(2, 8, 128), vm(2, 3, 8, 8, 128), vm(24, 48, 128), vm(24, 48, 128), vm(24, 48, 128),
        vm(16, 128), vm(64, 128), vm(10, 32, 128), vm(10, 24, 128), vm(10, 24, 128),
        vm(10, 32, 128), vm(10, 32, 128), vm(8, 16, 128), vm(8, 48, 128),
        vm(128, 128), vm(512, 384),
        vm(28, 48, 256), vm(16, 32, 128), vm(12, 24, 128), vm(16, 48, 128), vm(8, 32, 128),
        pltpu.SemaphoreType.DMA((N_SEMS,)), pltpu.SemaphoreType.DMA((N_SEMS,)),
    ]


def per_device(coarse_density, start_potential, pair_density, expansion, box_corners, box_offsets, lists, counts):
    del lists, counts
    block = jax.ShapeDtypeStruct((16, 32, 128), F32)
    vmem = pl.BlockSpec(memory_space=pltpu.VMEM)
    return pl.pallas_call(
        kernel,
        out_shape=(block, block),
        in_specs=[vmem] * 6,
        out_specs=(vmem, vmem),
        scratch_shapes=scratch(),
        compiler_params=pltpu.CompilerParams(
            collective_id=0, has_side_effects=True, vmem_limit_bytes=40 * 2**20
        ),
    )(coarse_density, start_potential, pair_density, expansion, box_corners, box_offsets)


def solution(mesh):
    everywhere = P(AXES, None)
    in_specs = (P(*AXES), P(*AXES), everywhere, P(), everywhere, everywhere, everywhere, P(AXES))
    return jax.shard_map(
        per_device, mesh=mesh, in_specs=in_specs, out_specs=(P(*AXES), P(*AXES)), check_vma=False
    )
```

time: 1050 us -> 94.2 us (0.09)
  the two profiles are of different devices: /device:TPU:228 before, /device:TPU:1 now
where the time goes in v1:
time: 94.2 us; the launch traced here: 93.9 us
  Pallas kernels  89.2 us (95%)
  local copies, waits for them, and re-layouts  4.06 us (4%)
    pallas_call x1, Pallas kernels, per_device(): pl.pallas_call(kernel, out_shape=(block, block), in_specs=[vmem] * 6, out...  89.2 us
    unnamed x13, local copies, waits for them, and re-layouts  4.06 us

profile of v1, /device:TPU:1, one launch (start us, length us, event | category | flops | bytes accessed | tf_op | source)
XLA Modules:
  0.0 93.9 jit_solution(8490034928861024602)
XLA Ops:
  0.6 0.0 copy-start.3
  0.6 0.0 copy-start.1
  0.6 0.8 copy.9.corner
  1.4 0.0 copy-done.3
  1.4 0.1 copy.10.offset
  1.5 0.0 copy-start.2
  1.5 0.8 copy.8.expn
  2.3 0.0 copy-done.1
  2.3 0.0 copy-done.2
  2.4 0.0 copy-start
  2.4 0.9 %copy-done = f32[16,32,128]{2,1,0:T(8,128)S(1)} copy-done((f32[16,32,128]{2,1,0:T(8,128)S(1)}, f32[16,32,128]{2,1,0:T(8,128)}, u32[]{:S(2)}) %copy-start) | copy-done | bytes 262168
  3.3 89.2 %shard_map.77 = (f32[16,32,128]{2,1,0:T(8,128)S(1)}, f32[16,32,128]{2,1,0:T(8,128)S(1)}) custom-call(f32[8,16,64]{2,1,0:T(8,128)S(1)} %copy-done.1, f32[16,32,128]{2,1,0:T(8,128)S(1)} %copy-done, f32[16,91]{1,0:T(8,128)S(1)} %copy-done.2, f32[91,9]{1,0:T(8,128)S(1)} %copy.8.expn, s32[16,3]{1,0:T(8,128)S(1)} %copy.9.corner, f32[16,3]{1,0:T(8,128)S(1)} %copy.10.offset), custom_call_target="tpu_custom_call" | custom-call | tf_op jit(solution)/shard_map/pallas_call | solution.py:567
  92.5 0.7 copy.13
  93.2 0.7 copy.14
Async XLA Ops:
  0.6 0.8 copy-start.3
  0.6 1.7 %copy-start.1 = (f32[8,16,64]{2,1,0:T(8,128)S(1)}, f32[8,16,64]{2,1,0:T(8,128)}, u32[]{:S(2)}) copy-start(f32[8,16,64]{2,1,0:T(8,128)} %rho.1) | copy-start | bytes 98308
  1.5 0.8 copy-start.2
  2.4 1.0 %copy-start = (f32[16,32,128]{2,1,0:T(8,128)S(1)}, f32[16,32,128]{2,1,0:T(8,128)}, u32[]{:S(2)}) copy-start(f32[16,32,128]{2,1,0:T(8,128)} %v0.1) | copy-start | bytes 786436

commit v2 on v1

v2 whole, which is shorter than its diff:
```python
import itertools

import jax
import jax.numpy as jnp
from jax import lax
from jax.experimental import pallas as pl
from jax.experimental.pallas import tpu as pltpu
from jax.sharding import PartitionSpec as P

F32 = jnp.float32
BF16 = jnp.bfloat16
MESH = pl.DeviceIdType.MESH
ALPHA = 0.8 / 6.0
AXES = ("gx", "gy", "gz")
DIRS = [d for d in itertools.product((-1, 0, 1), repeat=3) if d != (0, 0, 0)]
DIRS.sort(key=lambda d: -sum(map(abs, d)))
XY_DIRS = [d for d in DIRS if d[2] == 0 and d[0] != 0]
UP7 = [d for d in itertools.product((0, 1), repeat=3) if d != (0, 0, 0)]
RING = [4, 3, 5, 2, 6, 1, 7]
X_NEAR = [1, -1, 2, -2]
YZ_NEAR = [d for d in DIRS if d[0] == 0]
N_ATOM, N_DIR, N_RING = len(UP7), len(DIRS), len(RING)
SEM_V = N_ATOM
SEM_RHO = SEM_V + N_DIR
SEM_F = SEM_RHO + N_DIR
SEM_LATE = SEM_F + N_DIR
SEM_CYCLE = SEM_LATE + len(XY_DIRS)
PER_CYCLE = 2 * N_DIR + 2 * N_RING + len(X_NEAR) + len(YZ_NEAR)
N_SEMS = SEM_CYCLE + 2 * PER_CYCLE


def iota(shape, dim):
    return lax.broadcasted_iota(jnp.int32, shape, dim)


def wrapped(lane, cut, lanes):
    return jnp.where(lane < cut, lane, lane - lanes)


def split(a):
    hi = a.astype(BF16)
    return hi, (a - hi.astype(F32)).astype(BF16)


def dot(a, b):
    return jnp.dot(a, b, preferred_element_type=F32)


def mm(a, m):
    hi, lo = split(a)
    return dot(hi, m) + dot(lo, m)


def restrict_matrix(rows, rcut, cols, ccut):
    fine = wrapped(iota((rows, cols), 0), rcut, rows)
    coarse = wrapped(iota((rows, cols), 1), ccut, cols)
    return jnp.where((fine >> 1) == coarse, 1.0, 0.0).astype(BF16)


def prolong_matrix(rows, rcut, cols, ccut):
    coarse = wrapped(iota((rows, cols), 0), rcut, rows)
    fine = wrapped(iota((rows, cols), 1), ccut, cols)
    centre = fine >> 1
    other = jnp.where((fine & 1) == 0, centre - 1, centre + 1)
    return jnp.where(coarse == centre, 0.75, jnp.where(coarse == other, 0.25, 0.0)).astype(BF16)


def grid_mask(shape, starts, sizes, cut, window):
    x = iota(shape, 0) + starts[0]
    y = iota(shape, 1) + starts[1]
    z = wrapped(iota(shape, 2), cut, shape[2])
    near = (z >= window[0]) & (z < window[1])
    z = z + starts[2]
    inside = (x >= 0) & (x < sizes[0]) & (y >= 0) & (y < sizes[1]) & (z >= 0) & (z < sizes[2])
    return jnp.where(inside & near, 1.0, 0.0)


def neighbours(ref, first, count):
    c = ref[pl.ds(first, count)]
    rows, lanes = c.shape[1], c.shape[2]
    total = ref[pl.ds(first - 1, count)] + ref[pl.ds(first + 1, count)]
    total = total + pltpu.roll(c, 1, 1) + pltpu.roll(c, rows - 1, 1)
    return c, total + pltpu.roll(c, 1, 2) + pltpu.roll(c, lanes - 1, 2)


def expand_rows(es, ye, yo, r0, nr):
    def rows(start):
        return es[:, pl.ds(start, nr), :]

    mid = 0.75 * rows(r0)
    ye[...] = mid + 0.25 * rows(r0 - 1)
    yo[...] = mid + 0.25 * rows(r0 + 1)


def plane_pair(ye, yo, c0, k):
    pairs = []
    e, o = 0.75 * ye[k + c0], 0.75 * yo[k + c0]
    for side in (k + c0 - 1, k + c0 + 1):
        pairs.append((e + 0.25 * ye[side], o + 0.25 * yo[side]))
    return pairs


def expand_planes(ye, yo, out, f0, c0, k):
    for x, (even, odd) in enumerate(plane_pair(ye, yo, c0, k)):
        n = even.shape[0]
        out[f0 + 2 * k + x, pl.ds(0, n, 2), :] = even
        out[f0 + 2 * k + x, pl.ds(1, n, 2), :] = odd


def both(ref, i):
    return jnp.concatenate([ref[0, i], ref[1, i]], axis=1)


def spread(c, before, after):
    rows, lanes = c.shape
    total = before + after + pltpu.roll(c, 1, 0) + pltpu.roll(c, rows - 1, 0)
    return total + pltpu.roll(c, 1, 1) + pltpu.roll(c, lanes - 1, 1)


def halve_rows(ref, start, count):
    return ref[pl.ds(start, count, 2), :] + ref[pl.ds(start + 1, count, 2), :]


def kernel(
    rho_hbm, v0_hbm, pair, expn_t, corner_t, offset_t, dens, pot,
    vf, v1, ff, zl0, zh0, zs0, rho,
    f1, zl1, zh1, zs1, g1, a0, s0, es0, ye0, yo0, e1, w1, es1, ye1, yo1,
    t2, f2, e2, w2, s1, es2, ye2, yo2,
    x1, y1, f3, e3, w3, s2, a2, g3, s4, es3, ye3, yo3,
    xa, yb, ts, f4, v4,
    at, tp, pln, k0, ke, ko, k1, k2, k3, kg, k4, local, ss, rs,
):
    gx, gy, gz = (lax.axis_index(a) for a in AXES)
    here = (gx, gy, gz)

    def peer(d):
        return tuple(i if s == 0 else lax.rem(i + (s + 8), 8) for i, s in zip(here, d))

    rho_in = pltpu.make_async_copy(rho_hbm, rho, local.at[0])
    v0_in = pltpu.make_async_copy(v0_hbm, vf.at[6:22, 8:40, 0:128], local.at[1])
    rho_in.start()
    v0_in.start()
    barrier = pltpu.get_barrier_semaphore()
    reached = []
    for d in DIRS[::-1] + [(k, 0, 0) for k in RING] + [(0, k, 0) for k in RING]:
        d = tuple(s % 8 for s in d)
        if d not in reached:
            reached.append(d)
    for d in reached:
        pl.semaphore_signal(barrier, inc=1, device_id=peer(d), device_id_type=MESH)

    def pack0(frame, q):
        lane = iota((32, 128), 1)
        lo = hi = jnp.zeros((32, 128), F32)
        for x in range(16):
            t = frame[6 + x, 8:40, 0:128]
            if x:
                t = pltpu.roll(t, 8 * x, 1)
            h = (8 * x - 8) % 128
            lo = jnp.where((lane >= 8 * x) & (lane < 8 * x + 8), t, lo)
            hi = jnp.where((lane >= h) & (lane < h + 8), t, hi)
        zs0[q, 0] = lo
        zs0[q, 1] = hi

    def pack1(q):
        lane = iota((16, 128), 1)
        out = jnp.zeros((16, 128), F32)
        for x in range(8):
            t = f1[q, 4 + x, 8:24, :]
            lo = t if x == 0 else pltpu.roll(t, 16 * x, 1)
            hi = t if x == 3 else pltpu.roll(t, (16 * x - 48) % 128, 1)
            out = jnp.where((lane >= 16 * x) & (lane < 16 * x + 8), lo, out)
            out = jnp.where((lane >= 16 * x + 8) & (lane < 16 * x + 16), hi, out)
        zs1[q] = out

    hi_prec = lax.Precision.HIGHEST
    m = iota((9, 128), 0)
    c = iota((9, 128), 1)
    one = jnp.where((c < 7) & (m == c), 1.0, 0.0)
    one = one + jnp.where((c == 7) & (m == 7), 1.0, 0.0) - jnp.where((c == 7) & (m == 8), 1.0, 0.0)
    one = one - jnp.where((c == 8) & (m >= 7), 1.0, 0.0) + jnp.where((c == 9) & (m == 8), 2.0, 0.0)
    moments = lax.dot_general(
        pair[...], expn_t[...], (((1,), (1,)), ((), ())), precision=hi_prec, preferred_element_type=F32
    )
    packed = jnp.dot(moments, one, precision=hi_prec)
    corners = corner_t[...].astype(F32)
    tp[...] = jnp.zeros(tp.shape, F32)
    tp[10:13, 0:16] = corners + 5.5 + offset_t[...]
    tp[13:16, 0:16] = corners
    at[0:16, :] = packed + tp[...].T[0:16]
    rho_in.wait()
    f1[0, 4:12, 8:24, 0:64] = rho[...]
    pack1(0)
    v0_in.wait()
    pack0(vf, 0)

    pl.semaphore_wait(barrier, len(reached))

    def rcopy(src, dst, k, d):
        return pltpu.make_async_remote_copy(
            src_ref=src, dst_ref=dst, send_sem=ss.at[k], recv_sem=rs.at[k], device_id=peer(d), device_id_type=MESH
        )

    def atom_copies():
        return [
            rcopy(at.at[0:16], at.at[16 * k + 16 : 16 * k + 32], k, d) for k, d in enumerate(UP7)
        ]

    def frame_slices(d, nx, hx, ny, part):
        near, far = part
        src, dst = [], []
        for s, n, h, o, a, b in ((d[0], nx, hx, hx, near, far), (d[1], ny, 8, 8, 0, 8)):
            if s == 0:
                src.append(slice(o, o + n))
                dst.append(slice(o, o + n))
            elif s > 0:
                src.append(slice(o + n - b, o + n - a))
                dst.append(slice(h - b, h - a))
            else:
                src.append(slice(o + a, o + b))
                dst.append(slice(o + n + a, o + n + b))
        return tuple(src), tuple(dst)

    def copies0(frame, q, base, part):
        out = []
        for k, d in enumerate(DIRS):
            src, dst = frame_slices(d, 16, 6, 32, part)
            if d[2] == 0:
                out.append(rcopy(frame.at[src + (slice(0, 128),)], frame.at[dst + (slice(0, 128),)], base + k, d))
            else:
                rows = slice(src[1].start - 8, src[1].stop - 8)
                zr = zh0 if d[2] > 0 else zl0
                out.append(rcopy(zs0.at[q, 1 if d[2] > 0 else 0, rows], zr.at[q, 1 - d[0], dst[1]], base + k, d))
        return out

    def late_copies():
        out = []
        for k, d in enumerate(XY_DIRS):
            src, dst = frame_slices(d, 16, 6, 32, (3, 5))
            out.append(rcopy(ff.at[src + (slice(0, 128),)], ff.at[dst + (slice(0, 128),)], SEM_LATE + k, d))
        return out

    def copies1(q, base, part):
        out = []
        for k, d in enumerate(DIRS):
            src, dst = frame_slices(d, 8, 4, 16, part)
            if d[2] == 0:
                out.append(rcopy(f1.at[(q,) + src], f1.at[(q,) + dst], base + k, d))
            else:
                rows = slice(src[1].start - 8, src[1].stop - 8)
                zr = zh1 if d[2] > 0 else zl1
                out.append(rcopy(zs1.at[q, rows], zr.at[q, 1 - d[0], dst[1]], base + k, d))
        return out

    def copies2(q, base):
        mine = t2.at[q, 1, 1, 8:16]
        return [
            rcopy(mine, t2.at[q, 1 - d[2], 1 - d[0], 8 * (1 - d[1]) : 8 * (1 - d[1]) + 8], base + k, d)
            for k, d in enumerate(DIRS)
        ]

    def copies3a(q, base):
        return [rcopy(x1.at[q, 0], x1.at[q, k + 1], base + k, (n, 0, 0)) for k, n in enumerate(X_NEAR)]

    def copies3b(q, base):
        return [
            rcopy(y1.at[q, 1, 8:16], y1.at[q, 1 - d[2], 8 * (1 - d[1]) : 8 * (1 - d[1]) + 8], base + k, d)
            for k, d in enumerate(YZ_NEAR)
        ]

    def copies4a(q, base):
        return [rcopy(xa.at[q, gx], xa.at[q, gx], base + k, (n, 0, 0)) for k, n in enumerate(RING)]

    def copies4b(q, base):
        return [rcopy(yb.at[q, gy], yb.at[q, gy], base + k, (0, n, 0)) for k, n in enumerate(RING)]

    def start(copies):
        for item in copies:
            item.start()

    def wait_recv(copies):
        for item in copies:
            item.wait_recv()

    def wait_send(copies):
        for item in copies:
            item.wait_send()

    def in_x(i):
        x = 16 * gx + i - 6
        return jnp.where((x >= 0) & (x < 128), 1.0, 0.0)

    def unpack0(frame, q, halo, own):
        lane = iota((48, 128), 1)
        keep = (lane < 8) | (lane >= 120)

        def beside(slot, sx, i):
            t = jnp.where((lane >= 8 * sx) & (lane < 8 * sx + 8), zl0[q, slot], zh0[q, slot])
            t = pltpu.roll(t, lax.rem(128 - 8 * sx, 128), 1)
            return jnp.where(keep, t, 0.0) * (k0[:, 128:256] * in_x(i))

        for i in halo:
            below = i < 6
            frame[i, :, 0:128] = frame[i, :, 0:128] * (k0[:, 0:128] * in_x(i))
            frame[i, :, 128:256] = beside(0 if below else 2, jnp.int32(i + 10 if below else i - 22), i)

        def body(k, carry):
            values = [(i, beside(1, i - 6, i)) for i in (2 * k + 6, 2 * k + 7)]
            for i, value in values:
                frame[i, :, 128:256] = value
                for rows in (slice(0, 8), slice(40, 48)):
                    frame[i, rows, 0:128] = frame[i, rows, 0:128] * k0[rows, 0:128]
            return carry

        if own:
            lax.fori_loop(0, 8, body, 0)

    def unpack1(q):
        lane = iota((32, 128), 1)
        for i in range(16) if not isinstance(q, int) else range(3, 13):
            slot = 0 if i < 4 else 1 if i < 12 else 2
            sx = (4 + i) % 8 if i < 4 else (i - 4) % 8
            lo = zl1[q, slot]
            hi = zh1[q, slot]
            if (64 - 16 * sx) % 128:
                lo = pltpu.roll(lo, (64 - 16 * sx) % 128, 1)
            if (112 - 16 * sx) % 128:
                hi = pltpu.roll(hi, (112 - 16 * sx) % 128, 1)
            t = jnp.where(lane < 64, f1[q, i], jnp.where(lane < 72, lo, jnp.where(lane >= 120, hi, 0.0)))
            f1[q, i] = t * k1[i]

    def unpack2(q):
        lane = iota((24, 128), 1)
        for i in range(12):
            slot, sx = i // 4, i % 4
            below, mid, above = t2[q, 0, slot], t2[q, 1, slot], t2[q, 2, slot]
            if sx:
                mid = pltpu.roll(mid, 128 - 32 * sx, 1)
            if sx != 1:
                above = pltpu.roll(above, (32 - 32 * sx) % 128, 1)
            if sx != 3:
                below = pltpu.roll(below, 96 - 32 * sx, 1)
            t = jnp.where(lane < 32, mid, jnp.where(lane < 64, above, jnp.where(lane >= 96, below, 0.0)))
            f2[i] = t * k2[i]

    def unpack3(q):
        lane = iota((24, 128), 1)
        for dx in range(-2, 3):
            shift = 16 * lax.rem(gx + (dx + 8), 8)

            def turned(slot, target):
                return pltpu.roll(y1[q, slot], lax.rem(128 + target - shift, 128), 1)

            t = jnp.where(lane < 16, turned(1, 0), 0.0)
            t = jnp.where((lane >= 16) & (lane < 32), turned(2, 16), t)
            t = jnp.where(lane >= 112, turned(0, 112), t)
            for y in range(3):
                for x in range(2):
                    f3[2 * dx + 4 + x, 4 + 4 * y : 8 + 4 * y, :] = t[8 * y + 4 * x : 8 * y + 4 * x + 4]
        f3[...] = f3[...] * k3[...]

    def unpack4(q):
        lane = iota((64, 128), 1)
        for y in range(2):
            t = pltpu.roll(yb[q].reshape(64, 128), 120 - 32 * y, 1)
            ts[y] = jnp.where((lane < 16) | (lane >= 120), t, 0.0)
        for x in range(8):
            for y in range(2):
                f4[x, pl.ds(8 + y, 8, 2), :] = ts[y, pl.ds(x, 8, 8), :]

    def prolong0(source, first, add):
        es0[...] = mm(source.reshape(512, 128), prolong_matrix(128, 96, 256, 192)).reshape(16, 32, 256)

        def rows(i, carry):
            mid = 0.75 * es0[i, 4:28, :]
            even = (mid + 0.25 * es0[i, 3:27, :]) * ke[...]
            odd = (mid + 0.25 * es0[i, 5:29, :]) * ko[...]
            ye0[i] = even
            yo0[i] = odd
            return carry

        lax.fori_loop(first, 16 - first, rows, 0)

        def planes(k, carry):
            for x, pair_of in enumerate(plane_pair(ye0, yo0, 1, k)):
                i = 2 * k + x
                for y, value in enumerate(pair_of):
                    value = value * in_x(i)
                    for h in range(2):
                        at_rows = (h, i, pl.ds(y, 24, 2))
                        part = value[:, 128 * h : 128 * h + 128]
                        v1[at_rows] = v1[at_rows] + part if add else part
            return carry

        lax.fori_loop(first, 14 - first, planes, 0)

    atoms = atom_copies()
    start(atoms)
    rho_copies = copies1(0, SEM_RHO, (0, 1))
    start(rho_copies)
    v_copies = copies0(vf, 0, SEM_V, (0, 6))
    start(v_copies)

    for ref in (v1, g1, f3, e3, f4, v4, a2, w3):
        ref[...] = jnp.zeros(ref.shape, F32)
    k0[...] = grid_mask((1, 48, 256), (0, 32 * gy - 8, 128 * gz), (128, 256, 1024), 192, (-8, 136))[0]
    y_even = 2 * iota((24, 256), 0) + 32 * gy - 8
    z_at = wrapped(iota((24, 256), 1), 192, 256)
    z_in = (z_at >= -8) & (z_at < 136) & (z_at + 128 * gz >= 0) & (z_at + 128 * gz < 1024)
    y_in = (y_even >= 0) & (y_even < 256)
    ke[...] = jnp.where(y_in & z_in, 1.0, 0.0)
    ko[...] = ke[...]
    k1[...] = grid_mask((16, 32, 128), (8 * gx - 4, 16 * gy - 8, 64 * gz), (64, 128, 512), 96, (-8, 72))
    k2[...] = grid_mask((12, 24, 128), (4 * gx - 4, 8 * gy - 8, 32 * gz), (32, 64, 256), 96, (-32, 64))
    k3[...] = grid_mask((10, 24, 128), (2 * gx - 4, 4 * gy - 8, 16 * gz), (16, 32, 128), 64, (-16, 32))
    kg[...] = grid_mask((4, 16, 128), (2 * gx - 1, 4 * gy - 4, 16 * gz), (16, 32, 128), 64, (-16, 32))
    k4[...] = grid_mask((8, 32, 128), (0, -8, 8 * gz), (8, 16, 64), 64, (-8, 16))

    wait_send(rho_copies)
    wait_recv(rho_copies)
    unpack1(0)
    prolong0(f1[0], 3, False)

    wait_recv(atoms)
    by_atom = at[...]
    by_param = by_atom.T

    def factor(coord, centre, low):
        u = (coord - centre) * 0.5
        e = jnp.where((coord >= low) & (coord < low + 12.0), jnp.exp(-u * u), 0.0)
        return u, e

    def row(k):
        return by_param[k : k + 1, :]

    def coordinates(shape, dim, first):
        return (iota(shape, dim) + first).astype(F32)

    ux, ex = factor(coordinates((16, 128), 0, 16 * gx), row(10), row(13))
    uy, ey = factor(coordinates((32, 128), 0, 32 * gy), row(11), row(14))
    uz, ez = factor(coordinates((128, 128), 1, 128 * gz), by_atom[:, 12:13], by_atom[:, 15:16])
    uex = ux * ex
    p00 = row(0) * ex + row(1) * uex + row(7) * (ux * uex)
    p01 = row(2) * ex + row(4) * uex
    p02 = row(8) * ex
    p10 = row(3) * ex + row(6) * uex
    p11 = row(5) * ex
    p20 = row(9) * ex
    uey = uy * ey
    uuey = uy * uey
    for x in range(16):
        s = slice(x, x + 1)
        pln[32 * x : 32 * x + 32, 0:128] = p00[s] * ey + p01[s] * uey + p02[s] * uuey
        pln[32 * x : 32 * x + 32, 128:256] = p10[s] * ey + p11[s] * uey
        pln[32 * x : 32 * x + 32, 256:384] = p20[s] * ey
    uez = uz * ez
    z_hi, z_lo = split(jnp.concatenate([ez, uez, uz * uez], axis=0))
    p_hi, p_lo = split(pln[...])
    block = dot(p_hi, z_hi) + dot(p_hi, z_lo) + dot(p_lo, z_hi)
    block = block.reshape(16, 32, 128) + v1[0, 6:22, 8:40, :]
    dens[...] = block
    ff[6:22, 8:40, 0:128] = block

    pack0(ff, 1)
    f_copies = copies0(ff, 1, SEM_F, (0, 3))
    start(f_copies)
    late = late_copies()
    start(late)
    wait_send(v_copies)
    wait_recv(v_copies)
    unpack0(vf, 0, (*range(6), *range(22, 28)), True)
    wait_recv(f_copies)
    unpack0(ff, 1, (3, 4, 5, 22, 23, 24), True)

    def cycle(q, carry):
        base = SEM_CYCLE + q * PER_CYCLE
        c1 = copies1(q + 1, base, (0, 4))
        c2 = copies2(q, base + N_DIR)
        c4a = copies4a(q, base + 2 * N_DIR)
        c4b = copies4b(q, base + 2 * N_DIR + N_RING)
        c3a = copies3a(q, base + 2 * N_DIR + 2 * N_RING)
        c3b = copies3b(q, base + 2 * N_DIR + 2 * N_RING + len(X_NEAR))

        def pre(k, carry):
            values = []
            for i in (2 * k + 1, 2 * k + 2):
                c = vf[i]
                value = 0.2 * c + ALPHA * (ff[i] + spread(c, vf[i - 1], vf[i + 1]))
                values.append((i, value * (k0[...] * in_x(i))))
            for i, value in values:
                v1[0, i] = value[:, 0:128]
                v1[1, i] = value[:, 128:256]
            return carry

        lax.fori_loop(1, 12, pre, 0)

        def residual(k, carry):
            total = None
            for i in (2 * k + 4, 2 * k + 5):
                c = both(v1, i)
                r = ff[i] - 6.0 * c + spread(c, both(v1, i - 1), both(v1, i + 1))
                total = r if total is None else total + r
            s0[0] = total[:, 0:128]
            s0[1] = total[:, 128:256]
            a0[k] = jnp.concatenate([halve_rows(s0.at[h], 0, 24) for h in range(2)], axis=1)
            return carry

        lax.fori_loop(0, 10, residual, 0)
        g = 0.125 * mm(a0[...].reshape(240, 256), restrict_matrix(256, 192, 128, 96))
        g1[:, 4:28, :] = g.reshape(10, 24, 128)
        g1[...] = g1[...] * k1[3:13]
        f1[q + 1, 4:12, 8:24, :] = g1[1:9, 8:24, :]

        c, nb = neighbours(g1, 1, 8)
        r = (0.2 * c + ALPHA * nb).reshape(4, 2, 32, 128)
        s1[...] = r[:, 0] + r[:, 1]
        parts = jnp.concatenate(
            [s1[x, pl.ds(8, 8, 2), :] + s1[x, pl.ds(9, 8, 2), :] for x in range(4)], axis=1
        )
        row_at = iota((512, 128), 0)
        col_at = iota((512, 128), 1)
        lane_at = row_at & 127
        m2 = jnp.where((lane_at < 64) & ((row_at >> 7) * 32 + (lane_at >> 1) == col_at), 1.0, 0.0).astype(BF16)
        t2[q, 1, 1, 8:16] = 0.125 * mm(parts, m2)
        start(c2)
        pack1(q + 1)
        start(c1)

        wait_recv(c2)
        unpack2(q)
        c, nb = neighbours(f2, 2, 8)
        r = (0.2 * c + ALPHA * nb).reshape(4, 2, 24, 128)
        s2[...] = r[:, 0] + r[:, 1]
        a2[:, 0:12, :] = s2[:, pl.ds(0, 12, 2), :] + s2[:, pl.ds(1, 12, 2), :]
        g = 0.125 * mm(a2[...].reshape(64, 128), restrict_matrix(128, 96, 128, 64))
        g3[...] = g.reshape(4, 16, 128) * kg[...]
        c, nb = neighbours(g3, 1, 2)
        r = 0.2 * c + ALPHA * nb
        s4[...] = r[0] + r[1]
        parts = jnp.concatenate([s4[4:5] + s4[5:6], s4[6:7] + s4[7:8]], axis=1)
        row_at = iota((256, 128), 0)
        z_at = wrapped(row_at & 127, 64, 128) >> 1
        live = (z_at >= -8) & (z_at < 16) & (z_at + 8 * gz >= 0) & (z_at + 8 * gz < 64)
        m4 = jnp.where(live & (32 * (row_at >> 7) + z_at + 8 == iota((256, 128), 1)), 1.0, 0.0).astype(BF16)
        xa[q, gx] = 0.125 * mm(jnp.broadcast_to(parts, (8, 256)), m4)[0:1]
        start(c4a)
        tile = jnp.concatenate([g3[1, 4:8, :], g3[2, 4:8, :]], axis=0)
        x1[q, 0] = pltpu.roll(jnp.where(iota((8, 128), 1) < 16, tile, 0.0), 16 * gx, 1)
        start(c3a)
        wait_send(c2)
        wait_send(c1)
        wait_recv(c1)
        unpack1(q + 1)
        wait_recv(c4a)
        yb[q, gy] = xa[q].reshape(8, 128)
        start(c4b)
        wait_recv(c3a)
        total = x1[q, 0]
        for n in range(len(X_NEAR)):
            total = total + x1[q, n + 1]
        y1[q, 1, 8:16] = total
        start(c3b)
        wait_send(c4a)
        wait_send(c3a)

        @pl.when(q == 0)
        def _():
            wait_send(f_copies)
            wait_send(late)
            wait_recv(late)
            unpack0(ff, 1, (1, 2, 25, 26), False)
            pre(0, 0)
            pre(12, 0)

        wait_recv(c3b)
        unpack3(q)
        wait_recv(c4b)
        unpack4(q)

        weight4, weight3, weight2, weight1 = (ALPHA * 4.0**level for level in (4, 3, 2, 1))
        v4[4:12] = weight4 * f4[...]
        for _ in range(3):
            c, nb = neighbours(v4, 4, 8)
            v4[4:12] = (0.2 * c + ALPHA * nb + weight4 * f4[...]) * k4[...]

        near = v4[pl.ds(gx + 1, 7)].reshape(224, 128)
        es3[...] = mm(near, prolong_matrix(128, 64, 128, 64)).reshape(7, 32, 128)
        expand_rows(es3, ye3, yo3, 2 * gy + 4, 12)
        for k in range(5):
            expand_planes(ye3, yo3, w3, 0, 1, k)
        rhs = weight3 * f3[...]
        e3[...] = (rhs + w3[...]) * k3[...]
        c, nb = neighbours(e3, 1, 8)
        e3[1:9] = (0.2 * c + ALPHA * nb + rhs[1:9]) * k3[1:9]

        near = e3[1:9].reshape(192, 128)
        es2[...] = mm(near, prolong_matrix(128, 64, 128, 96)).reshape(8, 24, 128)
        expand_rows(es2, ye2, yo2, 4, 12)
        for k in range(6):
            expand_planes(ye2, yo2, w2, 0, 1, k)
        rhs = weight2 * f2[...]
        e2[...] = (rhs + w2[...]) * k2[...]
        c, nb = neighbours(e2, 1, 10)
        e2[1:11] = (0.2 * c + ALPHA * nb + rhs[1:11]) * k2[1:11]

        es1[...] = mm(e2[...].reshape(288, 128), prolong_matrix(128, 96, 128, 96)).reshape(12, 24, 128)
        expand_rows(es1, ye1, yo1, 4, 16)
        for k in range(8):
            expand_planes(ye1, yo1, w1, 0, 2, k)
        rhs = weight1 * f1[q + 1]
        e1[...] = (rhs + w1[...]) * k1[...]
        c, nb = neighbours(e1, 1, 14)
        e1[1:15] = (0.2 * c + ALPHA * nb + rhs[1:15]) * k1[1:15]

        prolong0(e1[...], 2 * q, True)

        def post(k, carry):
            values = []
            for i in (2 * k + 2, 2 * k + 3):
                c = both(v1, i)
                value = 0.2 * c + ALPHA * (ff[i] + spread(c, both(v1, i - 1), both(v1, i + 1)))
                values.append((i, value * (k0[...] * in_x(i))))
            for i, value in values:
                vf[i] = value
            return carry

        lax.fori_loop(2 * q, 12 - 2 * q, post, 0)
        wait_send(c4b)
        wait_send(c3b)
        return carry

    lax.fori_loop(0, 2, cycle, 0)
    pot[...] = vf[6:22, 8:40, 0:128]
    wait_send(atoms)


def scratch():
    def vm(*shape):
        return pltpu.VMEM(shape, F32)

    return [
        vm(28, 48, 256), vm(2, 28, 48, 128), vm(28, 48, 256),
        vm(2, 3, 48, 128), vm(2, 3, 48, 128), vm(2, 2, 32, 128), vm(8, 16, 64),
        vm(3, 16, 32, 128), vm(3, 3, 32, 128), vm(3, 3, 32, 128), vm(3, 16, 128),
        vm(10, 32, 128), vm(10, 24, 256), vm(2, 48, 128), vm(16, 32, 256), vm(16, 24, 256), vm(16, 24, 256),
        vm(16, 32, 128), vm(16, 32, 128), vm(12, 24, 128), vm(12, 16, 128), vm(12, 16, 128),
        vm(2, 3, 3, 24, 128), vm(12, 24, 128), vm(12, 24, 128), vm(12, 24, 128), vm(4, 32, 128),
        vm(8, 24, 128), vm(8, 12, 128), vm(8, 12, 128),
        vm(2, 5, 8, 128), vm(2, 3, 24, 128), vm(10, 24, 128), vm(10, 24, 128), vm(10, 24, 128),
        vm(4, 24, 128), vm(4, 16, 128), vm(4, 16, 128), vm(16, 128), vm(7, 32, 128), vm(7, 12, 128), vm(7, 12, 128),
        vm(2, 8, 1, 128), vm(2, 8, 8, 128), vm(2, 64, 128), vm(8, 32, 128), vm(16, 32, 128),
        vm(128, 128), vm(128, 128), vm(512, 384),
        vm(48, 256), vm(24, 256), vm(24, 256),
        vm(16, 32, 128), vm(12, 24, 128), vm(10, 24, 128), vm(4, 16, 128), vm(8, 32, 128),
        pltpu.SemaphoreType.DMA((2,)), pltpu.SemaphoreType.DMA((N_SEMS,)), pltpu.SemaphoreType.DMA((N_SEMS,)),
    ]


def per_device(coarse_density, start_potential, pair_density, expansion, box_corners, box_offsets, lists, counts):
    del lists, counts
    block = jax.ShapeDtypeStruct((16, 32, 128), F32)
    vmem = pl.BlockSpec(memory_space=pltpu.VMEM)
    hbm = pl.BlockSpec(memory_space=pltpu.HBM)
    return pl.pallas_call(
        kernel,
        out_shape=(block, block),
        in_specs=[hbm] * 2 + [vmem] * 4,
        out_specs=(vmem, vmem),
        scratch_shapes=scratch(),
        compiler_params=pltpu.CompilerParams(
            collective_id=0, has_side_effects=True, vmem_limit_bytes=40 * 2**20
        ),
    )(coarse_density, start_potential, pair_density, expansion.T, box_corners.T, box_offsets.T)


def solution(mesh):
    everywhere = P(AXES, None)
    in_specs = (P(*AXES), P(*AXES), everywhere, P(), everywhere, everywhere, everywhere, P(AXES))
    return jax.shard_map(
        per_device, mesh=mesh, in_specs=in_specs, out_specs=(P(*AXES), P(*AXES)), check_vma=False
    )
```

time: 94.2 us -> 81.1 us (0.86)
  Pallas kernels: 89.2 us -> 74.8 us
  local copies, waits for them, and re-layouts: 4.06 us -> 5.27 us
    pallas_call x1, Pallas kernels: 89.2 us -> 74.8 us  [per_device(): pl.pallas_call(kernel, out_shape=(block, block), in_specs=[hbm] * 2 + [vm...]
    unnamed x13 -> x14, local copies, waits for them, and re-layouts: 4.06 us -> 5.27 us
where the time goes in v2:
time: 81.1 us; the launch traced here: 80.8 us
  Pallas kernels  74.8 us (92%)
  local copies, waits for them, and re-layouts  5.27 us (6%)
    pallas_call x1, Pallas kernels, per_device(): pl.pallas_call(kernel, out_shape=(block, block), in_specs=[hbm] * 2 + [vm...  74.8 us
    unnamed x14, local copies, waits for them, and re-layouts  5.27 us

profile of v2, /device:TPU:1, one launch (start us, length us, event | category | flops | bytes accessed | tf_op | source)
XLA Modules:
  0.0 80.8 jit_solution(15942303722229667259)
XLA Ops:
  0.6 0.0 copy-start.5
  0.6 0.0 copy-start.4
  0.7 0.7 copy-done.5
  1.3 0.0 copy-done.4
  1.3 0.0 copy-start
  1.3 0.9 %copy-done = f32[16,32,128]{2,1,0:T(8,128)S(1)} copy-done((f32[16,32,128]{2,1,0:T(8,128)S(1)}, f32[16,32,128]{2,1,0:T(8,128)}, u32[]{:S(2)}) %copy-start) | copy-done | bytes 262168
  2.3 0.0 copy-start.1
  2.3 0.8 %copy-done.1 = f32[8,16,64]{2,1,0:T(8,128)S(1)} copy-done((f32[8,16,64]{2,1,0:T(8,128)S(1)}, f32[8,16,64]{2,1,0:T(8,128)}, u32[]{:S(2)}) %copy-start.1) | copy-done | bytes 32792
  3.1 0.0 copy-start.2
  3.1 0.7 copy-done.2
  3.8 0.0 copy-start.3
  3.8 0.7 copy-done.3
  4.5 74.8 %shard_map.77 = (f32[16,32,128]{2,1,0:T(8,128)S(1)}, f32[16,32,128]{2,1,0:T(8,128)S(1)}) custom-call(f32[8,16,64]{2,1,0:T(8,128)S(1)} %copy-done.1, f32[16,32,128]{2,1,0:T(8,128)S(1)} %copy-done, f32[16,91]{1,0:T(8,128)S(1)} %copy-done.2, f32[9,91]{1,0:T(8,128)S(1)} %bitcast.3, s32[3,16]{1,0:T(4,128)S(1)} %bitcast.4, f32[3,16]{1,0:T(4,128)S(1)} %bitcast.5), custom_call_target="tpu_custom_call" | custom-call | tf_op jit(solution)/shard_map/pallas_call | solution.py:664
  79.4 0.7 copy.10
  80.1 0.7 copy.11
Async XLA Ops:
  0.6 0.7 copy-start.5
  0.6 0.7 copy-start.4
  1.3 0.9 %copy-start = (f32[16,32,128]{2,1,0:T(8,128)S(1)}, f32[16,32,128]{2,1,0:T(8,128)}, u32[]{:S(2)}) copy-start(f32[16,32,128]{2,1,0:T(8,128)} %v0_hbm.1) | copy-start | bytes 786436
  2.3 0.8 %copy-start.1 = (f32[8,16,64]{2,1,0:T(8,128)S(1)}, f32[8,16,64]{2,1,0:T(8,128)}, u32[]{:S(2)}) copy-start(f32[8,16,64]{2,1,0:T(8,128)} %rho_hbm.1) | copy-start | bytes 98308
  3.1 0.7 copy-start.2
  3.8 0.7 copy-start.3

commit v3 on v2

--- a/solution.py
+++ b/solution.py
@@ -122,8 +122,8 @@
 
 
 def kernel(
-    rho_hbm, v0_hbm, pair, expn_t, corner_t, offset_t, dens, pot,
-    vf, v1, ff, zl0, zh0, zs0, rho,
+    rho_hbm, v0_hbm, pair_hbm, expn_hbm, corner_hbm, offset_hbm, dens, pot,
+    pair, expn_t, corner_t, offset_t, vf, v1, ff, zl0, zh0, zs0, rho,
     f1, zl1, zh1, zs1, g1, a0, s0, es0, ye0, yo0, e1, w1, es1, ye1, yo1,
     t2, f2, e2, w2, s1, es2, ye2, yo2,
     x1, y1, f3, e3, w3, s2, a2, g3, s4, es3, ye3, yo3,
@@ -138,8 +138,14 @@
 
     rho_in = pltpu.make_async_copy(rho_hbm, rho, local.at[0])
     v0_in = pltpu.make_async_copy(v0_hbm, vf.at[6:22, 8:40, 0:128], local.at[1])
-    rho_in.start()
-    v0_in.start()
+    small_in = [
+        pltpu.make_async_copy(src, dst, local.at[2 + k])
+        for k, (src, dst) in enumerate(
+            ((pair_hbm, pair), (expn_hbm, expn_t), (corner_hbm, corner_t), (offset_hbm, offset_t))
+        )
+    ]
+    for item in [rho_in, v0_in] + small_in:
+        item.start()
     barrier = pltpu.get_barrier_semaphore()
     reached = []
     for d in DIRS[::-1] + [(k, 0, 0) for k in RING] + [(0, k, 0) for k in RING]:
@@ -179,6 +185,8 @@
     one = jnp.where((c < 7) & (m == c), 1.0, 0.0)
     one = one + jnp.where((c == 7) & (m == 7), 1.0, 0.0) - jnp.where((c == 7) & (m == 8), 1.0, 0.0)
     one = one - jnp.where((c == 8) & (m >= 7), 1.0, 0.0) + jnp.where((c == 9) & (m == 8), 2.0, 0.0)
+    for item in small_in:
+        item.wait()
     moments = lax.dot_general(
         pair[...], expn_t[...], (((1,), (1,)), ((), ())), precision=hi_prec, preferred_element_type=F32
     )
@@ -481,31 +489,36 @@
         c3a = copies3a(q, base + 2 * N_DIR + 2 * N_RING)
         c3b = copies3b(q, base + 2 * N_DIR + 2 * N_RING + len(X_NEAR))
 
-        def pre(k, carry):
+        def pre(first, count):
             values = []
-            for i in (2 * k + 1, 2 * k + 2):
+            for i in [first + j for j in range(count)]:
                 c = vf[i]
                 value = 0.2 * c + ALPHA * (ff[i] + spread(c, vf[i - 1], vf[i + 1]))
                 values.append((i, value * (k0[...] * in_x(i))))
             for i, value in values:
                 v1[0, i] = value[:, 0:128]
                 v1[1, i] = value[:, 128:256]
-            return carry
-
-        lax.fori_loop(1, 12, pre, 0)
-
-        def residual(k, carry):
-            total = None
-            for i in (2 * k + 4, 2 * k + 5):
-                c = both(v1, i)
-                r = ff[i] - 6.0 * c + spread(c, both(v1, i - 1), both(v1, i + 1))
-                total = r if total is None else total + r
-            s0[0] = total[:, 0:128]
-            s0[1] = total[:, 128:256]
-            a0[k] = jnp.concatenate([halve_rows(s0.at[h], 0, 24) for h in range(2)], axis=1)
-            return carry
-
-        lax.fori_loop(0, 10, residual, 0)
+
+        @pl.loop(0, 2)
+        def _(k):
+            pre(11 * k + 3, 11)
+
+        @pl.loop(0, 5)
+        def _(k):
+            sums = []
+            for pair_at in (2 * k, 2 * k + 1):
+                total = None
+                for i in (2 * pair_at + 4, 2 * pair_at + 5):
+                    c = both(v1, i)
+                    r = ff[i] - 6.0 * c + spread(c, both(v1, i - 1), both(v1, i + 1))
+                    total = r if total is None else total + r
+                sums.append((pair_at, total))
+            for n, (_, total) in enumerate(sums):
+                s0[n, 0] = total[:, 0:128]
+                s0[n, 1] = total[:, 128:256]
+            for n, (pair_at, _) in enumerate(sums):
+                a0[pair_at] = jnp.concatenate([halve_rows(s0.at[n, h], 0, 24) for h in range(2)], axis=1)
+
         g = 0.125 * mm(a0[...].reshape(240, 256), restrict_matrix(256, 192, 128, 96))
         g1[:, 4:28, :] = g.reshape(10, 24, 128)
         g1[...] = g1[...] * k1[3:13]
@@ -569,8 +582,8 @@
             wait_send(late)
             wait_recv(late)
             unpack0(ff, 1, (1, 2, 25, 26), False)
-            pre(0, 0)
-            pre(12, 0)
+            pre(1, 2)
+            pre(25, 2)
 
         wait_recv(c3b)
         unpack3(q)
@@ -616,7 +629,7 @@
 
         def post(k, carry):
             values = []
-            for i in (2 * k + 2, 2 * k + 3):
+            for i in [8 * k + 4 * q + 2 + j for j in range(8)]:
                 c = both(v1, i)
                 value = 0.2 * c + ALPHA * (ff[i] + spread(c, both(v1, i - 1), both(v1, i + 1)))
                 values.append((i, value * (k0[...] * in_x(i))))
@@ -624,7 +637,7 @@
                 vf[i] = value
             return carry
 
-        lax.fori_loop(2 * q, 12 - 2 * q, post, 0)
+        lax.fori_loop(0, 3 - q, post, 0)
         wait_send(c4b)
         wait_send(c3b)
         return carry
@@ -639,10 +652,11 @@
         return pltpu.VMEM(shape, F32)
 
     return [
+        vm(16, 91), vm(9, 91), pltpu.VMEM((3, 16), jnp.int32), vm(3, 16),
         vm(28, 48, 256), vm(2, 28, 48, 128), vm(28, 48, 256),
         vm(2, 3, 48, 128), vm(2, 3, 48, 128), vm(2, 2, 32, 128), vm(8, 16, 64),
         vm(3, 16, 32, 128), vm(3, 3, 32, 128), vm(3, 3, 32, 128), vm(3, 16, 128),
-        vm(10, 32, 128), vm(10, 24, 256), vm(2, 48, 128), vm(16, 32, 256), vm(16, 24, 256), vm(16, 24, 256),
+        vm(10, 32, 128), vm(10, 24, 256), vm(2, 2, 48, 128), vm(16, 32, 256), vm(16, 24, 256), vm(16, 24, 256),
         vm(16, 32, 128), vm(16, 32, 128), vm(12, 24, 128), vm(12, 16, 128), vm(12, 16, 128),
         vm(2, 3, 3, 24, 128), vm(12, 24, 128), vm(12, 24, 128), vm(12, 24, 128), vm(4, 32, 128),
         vm(8, 24, 128), vm(8, 12, 128), vm(8, 12, 128),
@@ -652,7 +666,7 @@
         vm(128, 128), vm(128, 128), vm(512, 384),
         vm(48, 256), vm(24, 256), vm(24, 256),
         vm(16, 32, 128), vm(12, 24, 128), vm(10, 24, 128), vm(4, 16, 128), vm(8, 32, 128),
-        pltpu.SemaphoreType.DMA((2,)), pltpu.SemaphoreType.DMA((N_SEMS,)), pltpu.SemaphoreType.DMA((N_SEMS,)),
+        pltpu.SemaphoreType.DMA((6,)), pltpu.SemaphoreType.DMA((N_SEMS,)), pltpu.SemaphoreType.DMA((N_SEMS,)),
     ]
 
 
@@ -664,11 +678,11 @@
     return pl.pallas_call(
         kernel,
         out_shape=(block, block),
-        in_specs=[hbm] * 2 + [vmem] * 4,
+        in_specs=[hbm] * 6,
         out_specs=(vmem, vmem),
         scratch_shapes=scratch(),
         compiler_params=pltpu.CompilerParams(
-            collective_id=0, has_side_effects=True, vmem_limit_bytes=40 * 2**20
+            collective_id=0, has_side_effects=True, vmem_limit_bytes=64 * 2**20
         ),
     )(coarse_density, start_potential, pair_density, expansion.T, box_corners.T, box_offsets.T)
 

time: 81.1 us -> 75.9 us (0.936)
  local copies, waits for them, and re-layouts: 5.27 us -> 2.42 us
  Pallas kernels: 74.8 us -> 72.7 us
    unnamed x14 -> x4, local copies, waits for them, and re-layouts: 5.27 us -> 2.42 us
    pallas_call x1, Pallas kernels: 74.8 us -> 72.7 us  [per_device(): pl.pallas_call(kernel, out_shape=(block, block), in_specs=[hbm] * 6, out_...]
where the time goes in v3:
time: 75.9 us; the launch traced here: 75.8 us
  Pallas kernels  72.7 us (96%)
  local copies, waits for them, and re-layouts  2.42 us (3%)
    pallas_call x1, Pallas kernels, per_device(): pl.pallas_call(kernel, out_shape=(block, block), in_specs=[hbm] * 6, out_...  72.7 us
    unnamed x4, local copies, waits for them, and re-layouts  2.42 us

profile of v3, /device:TPU:1, one launch (start us, length us, event | category | flops | bytes accessed | tf_op | source)
XLA Modules:
  0.0 75.8 jit_solution(6720524043762353680)
XLA Ops:
  0.6 72.7 %shard_map.77 = (f32[16,32,128]{2,1,0:T(8,128)}, f32[16,32,128]{2,1,0:T(8,128)}) custom-call(f32[8,16,64]{2,1,0:T(8,128)} %rho_hbm.1, f32[16,32,128]{2,1,0:T(8,128)} %v0_hbm.1, f32[16,91]{1,0:T(8,128)} %pair_hbm.1, f32[9,91]{1,0:T(8,128)} %bitcast.3, s32[3,16]{1,0:T(4,128)} %bitcast.4, f32[3,16]{1,0:T(4,128)} %bitcast.5), custom_call_target="tpu_custom_call" | custom-call | tf_op jit(solution)/shard_map/pallas_call | solution.py:678
  73.3 0.0 copy-start
  73.3 1.7 %copy.10 = f32[16,32,128]{2,1,0:T(8,128)} copy(f32[16,32,128]{2,1,0:T(8,128)} %get-tuple-element.4) | data formatting | bytes 524288
  75.1 0.0 copy-done
  75.1 0.7 copy.11
Async XLA Ops:
  73.3 1.7 %copy-start = (f32[16,32,128]{2,1,0:T(8,128)S(1)}, f32[16,32,128]{2,1,0:T(8,128)}, u32[]{:S(2)}) copy-start(f32[16,32,128]{2,1,0:T(8,128)} %get-tuple-element.5) | copy-start | bytes 786436

commit v4 on v3

--- a/solution.py
+++ b/solution.py
@@ -122,8 +122,8 @@
 
 
 def kernel(
-    rho_hbm, v0_hbm, pair_hbm, expn_hbm, corner_hbm, offset_hbm, dens, pot,
-    pair, expn_t, corner_t, offset_t, vf, v1, ff, zl0, zh0, zs0, rho,
+    rho_hbm, v0_hbm, pair_hbm, expn_hbm, corner_hbm, offset_hbm, smooth_out, local_out, sweep_out,
+    smooth, gauss, pair, expn_t, corner_t, offset_t, vf, v1, ff, zl0, zh0, zs0, rho,
     f1, zl1, zh1, zs1, g1, a0, s0, es0, ye0, yo0, e1, w1, es1, ye1, yo1,
     t2, f2, e2, w2, s1, es2, ye2, yo2,
     x1, y1, f3, e3, w3, s2, a2, g3, s4, es3, ye3, yo3,
@@ -313,7 +313,7 @@
             frame[i, :, 128:256] = beside(0 if below else 2, jnp.int32(i + 10 if below else i - 22), i)
 
         def body(k, carry):
-            values = [(i, beside(1, i - 6, i)) for i in (2 * k + 6, 2 * k + 7)]
+            values = [(i, beside(1, i - 6, i)) for i in [4 * k + 6 + j for j in range(4)]]
             for i, value in values:
                 frame[i, :, 128:256] = value
                 for rows in (slice(0, 8), slice(40, 48)):
@@ -321,7 +321,7 @@
             return carry
 
         if own:
-            lax.fori_loop(0, 8, body, 0)
+            lax.fori_loop(0, 4, body, 0)
 
     def unpack1(q):
         lane = iota((32, 128), 1)
@@ -379,28 +379,33 @@
     def prolong0(source, first, add):
         es0[...] = mm(source.reshape(512, 128), prolong_matrix(128, 96, 256, 192)).reshape(16, 32, 256)
 
-        def rows(i, carry):
-            mid = 0.75 * es0[i, 4:28, :]
-            even = (mid + 0.25 * es0[i, 3:27, :]) * ke[...]
-            odd = (mid + 0.25 * es0[i, 5:29, :]) * ko[...]
-            ye0[i] = even
-            yo0[i] = odd
+        def rows(k, carry):
+            values = []
+            for i in (first + 2 * k, first + 2 * k + 1):
+                mid = 0.75 * es0[i, 4:28, :]
+                even = (mid + 0.25 * es0[i, 3:27, :]) * ke[...]
+                odd = (mid + 0.25 * es0[i, 5:29, :]) * ko[...]
+                values.append((i, even, odd))
+            for i, even, odd in values:
+                ye0[i] = even
+                yo0[i] = odd
             return carry
 
-        lax.fori_loop(first, 16 - first, rows, 0)
-
-        def planes(k, carry):
-            for x, pair_of in enumerate(plane_pair(ye0, yo0, 1, k)):
-                i = 2 * k + x
-                for y, value in enumerate(pair_of):
-                    value = value * in_x(i)
-                    for h in range(2):
-                        at_rows = (h, i, pl.ds(y, 24, 2))
-                        part = value[:, 128 * h : 128 * h + 128]
-                        v1[at_rows] = v1[at_rows] + part if add else part
+        lax.fori_loop(0, 8 - first, rows, 0)
+
+        def planes(step, carry):
+            for k in (first + 2 * step, first + 2 * step + 1):
+                for x, pair_of in enumerate(plane_pair(ye0, yo0, 1, k)):
+                    i = 2 * k + x
+                    for y, value in enumerate(pair_of):
+                        value = value * in_x(i)
+                        for h in range(2):
+                            at_rows = (h, i, pl.ds(y, 24, 2))
+                            part = value[:, 128 * h : 128 * h + 128]
+                            v1[at_rows] = v1[at_rows] + part if add else part
             return carry
 
-        lax.fori_loop(first, 14 - first, planes, 0)
+        lax.fori_loop(0, 7 - first, planes, 0)
 
     atoms = atom_copies()
     start(atoms)
@@ -465,15 +470,20 @@
     z_hi, z_lo = split(jnp.concatenate([ez, uez, uz * uez], axis=0))
     p_hi, p_lo = split(pln[...])
     block = dot(p_hi, z_hi) + dot(p_hi, z_lo) + dot(p_lo, z_hi)
-    block = block.reshape(16, 32, 128) + v1[0, 6:22, 8:40, :]
-    dens[...] = block
-    ff[6:22, 8:40, 0:128] = block
+    gauss[...] = block.reshape(16, 32, 128)
+    smooth[...] = v1[0, 6:22, 8:40, :]
+    ff[6:22, 8:40, 0:128] = smooth[...] + gauss[...]
+    parts_out = [
+        pltpu.make_async_copy(smooth, smooth_out, local.at[6]),
+        pltpu.make_async_copy(gauss, local_out, local.at[7]),
+    ]
 
     pack0(ff, 1)
     f_copies = copies0(ff, 1, SEM_F, (0, 3))
     start(f_copies)
     late = late_copies()
     start(late)
+    start(parts_out)
     wait_send(v_copies)
     wait_recv(v_copies)
     unpack0(vf, 0, (*range(6), *range(22, 28)), True)
@@ -627,11 +637,13 @@
 
         prolong0(e1[...], 2 * q, True)
 
+        source = jnp.where(q == 0, 1.0, 0.0)
+
         def post(k, carry):
             values = []
             for i in [8 * k + 4 * q + 2 + j for j in range(8)]:
                 c = both(v1, i)
-                value = 0.2 * c + ALPHA * (ff[i] + spread(c, both(v1, i - 1), both(v1, i + 1)))
+                value = 0.2 * c + ALPHA * (source * ff[i] + spread(c, both(v1, i - 1), both(v1, i + 1)))
                 values.append((i, value * (k0[...] * in_x(i))))
             for i, value in values:
                 vf[i] = value
@@ -643,8 +655,12 @@
         return carry
 
     lax.fori_loop(0, 2, cycle, 0)
-    pot[...] = vf[6:22, 8:40, 0:128]
+    result = pltpu.make_async_copy(vf.at[6:22, 8:40, 0:128], sweep_out, local.at[8])
+    result.start()
     wait_send(atoms)
+    for item in parts_out:
+        item.wait()
+    result.wait()
 
 
 def scratch():
@@ -652,7 +668,7 @@
         return pltpu.VMEM(shape, F32)
 
     return [
-        vm(16, 91), vm(9, 91), pltpu.VMEM((3, 16), jnp.int32), vm(3, 16),
+        vm(16, 32, 128), vm(16, 32, 128), vm(16, 91), vm(9, 91), pltpu.VMEM((3, 16), jnp.int32), vm(3, 16),
         vm(28, 48, 256), vm(2, 28, 48, 128), vm(28, 48, 256),
         vm(2, 3, 48, 128), vm(2, 3, 48, 128), vm(2, 2, 32, 128), vm(8, 16, 64),
         vm(3, 16, 32, 128), vm(3, 3, 32, 128), vm(3, 3, 32, 128), vm(3, 16, 128),
@@ -666,25 +682,26 @@
         vm(128, 128), vm(128, 128), vm(512, 384),
         vm(48, 256), vm(24, 256), vm(24, 256),
         vm(16, 32, 128), vm(12, 24, 128), vm(10, 24, 128), vm(4, 16, 128), vm(8, 32, 128),
-        pltpu.SemaphoreType.DMA((6,)), pltpu.SemaphoreType.DMA((N_SEMS,)), pltpu.SemaphoreType.DMA((N_SEMS,)),
+        pltpu.SemaphoreType.DMA((9,)), pltpu.SemaphoreType.DMA((N_SEMS,)), pltpu.SemaphoreType.DMA((N_SEMS,)),
     ]
 
 
 def per_device(coarse_density, start_potential, pair_density, expansion, box_corners, box_offsets, lists, counts):
     del lists, counts
     block = jax.ShapeDtypeStruct((16, 32, 128), F32)
-    vmem = pl.BlockSpec(memory_space=pltpu.VMEM)
     hbm = pl.BlockSpec(memory_space=pltpu.HBM)
-    return pl.pallas_call(
+    smooth, gauss, sweep = pl.pallas_call(
         kernel,
-        out_shape=(block, block),
+        out_shape=(block, block, block),
         in_specs=[hbm] * 6,
-        out_specs=(vmem, vmem),
+        out_specs=(hbm, hbm, hbm),
         scratch_shapes=scratch(),
         compiler_params=pltpu.CompilerParams(
             collective_id=0, has_side_effects=True, vmem_limit_bytes=64 * 2**20
         ),
     )(coarse_density, start_potential, pair_density, expansion.T, box_corners.T, box_offsets.T)
+    total_density = smooth + gauss
+    return total_density, sweep + ALPHA * total_density
 
 
 def solution(mesh):

time: 75.9 us -> 74.9 us (0.987)
  local copies, waits for them, and re-layouts: 2.42 us -> 0 us
  other arithmetic: 0 us -> 1.96 us
    unnamed x4 -> x0, local copies, waits for them, and re-layouts: 2.42 us -> none
    add x0 -> x1, other arithmetic: none -> 1.96 us  [per_device(): return (total_density, sweep + ALPHA * total_density)]
where the time goes in v4:
time: 74.9 us; the launch traced here: 74.8 us
  Pallas kernels  72.2 us (96%)
  other arithmetic  1.96 us (3%)
    pallas_call x1, Pallas kernels, per_device(): pl.pallas_call(kernel, out_shape=(block, block, block), in_specs=[hbm] *...  72.2 us
    add x1, other arithmetic, per_device(): return (total_density, sweep + ALPHA * total_density)  1.96 us

profile of v4, /device:TPU:1, one launch (start us, length us, event | category | flops | bytes accessed | tf_op | source)
XLA Modules:
  0.0 74.8 jit_solution(8378669378224025460)
XLA Ops:
  0.6 72.2 %shard_map.77 = (f32[16,32,128]{2,1,0:T(8,128)}, f32[16,32,128]{2,1,0:T(8,128)}, f32[16,32,128]{2,1,0:T(8,128)}) custom-call(f32[8,16,64]{2,1,0:T(8,128)} %rho_hbm.1, f32[16,32,128]{2,1,0:T(8,128)} %v0_hbm.1, f32[16,91]{1,0:T(8,128)} %pair_hbm.1, f32[9,91]{1,0:T(8,128)} %bitcast.3, s32[3,16]{1,0:T(4,128)} %bitcast.4, f32[3,16]{1,0:T(4,128)} %bitcast.5), custom_call_target="tpu_custom_call" | custom-call | tf_op jit(solution)/shard_map/pallas_call | solution.py:693
  72.8 2.0 %multiply_add_fusion = (f32[16,32,128]{2,1,0:T(8,128)}, f32[16,32,128]{2,1,0:T(8,128)}) fusion(f32[16,32,128]{2,1,0:T(8,128)} %get-tuple-element.7, f32[16,32,128]{2,1,0:T(8,128)} %get-tuple-element.5, f32[16,32,128]{2,1,0:T(8,128)} %get-tuple-element.6), kind=kLoop, calls=%fused_computation | loop fusion | flops 196608 | bytes 1310720 | tf_op jit(solution)/shard_map/add | solution.py:704

commit v5 on v4

--- a/solution.py
+++ b/solution.py
@@ -179,6 +179,217 @@
             out = jnp.where((lane >= 16 * x + 8) & (lane < 16 * x + 16), hi, out)
         zs1[q] = out
 
+    rho_in.wait()
+    f1[0, 4:12, 8:24, 0:64] = rho[...]
+    pack1(0)
+
+    pl.semaphore_wait(barrier, len(reached))
+
+    def rcopy(src, dst, k, d):
+        return pltpu.make_async_remote_copy(
+            src_ref=src, dst_ref=dst, send_sem=ss.at[k], recv_sem=rs.at[k], device_id=peer(d), device_id_type=MESH
+        )
+
+    def atom_copies():
+        return [
+            rcopy(at.at[0:16], at.at[16 * k + 16 : 16 * k + 32], k, d) for k, d in enumerate(UP7)
+        ]
+
+    def frame_slices(d, nx, hx, ny, part):
+        near, far = part
+        src, dst = [], []
+        for s, n, h, o, a, b in ((d[0], nx, hx, hx, near, far), (d[1], ny, 8, 8, 0, 8)):
+            if s == 0:
+                src.append(slice(o, o + n))
+                dst.append(slice(o, o + n))
+            elif s > 0:
+                src.append(slice(o + n - b, o + n - a))
+                dst.append(slice(h - b, h - a))
+            else:
+                src.append(slice(o + a, o + b))
+                dst.append(slice(o + n + a, o + n + b))
+        return tuple(src), tuple(dst)
+
+    def copies0(frame, q, base, part):
+        out = []
+        for k, d in enumerate(DIRS):
+            src, dst = frame_slices(d, 16, 6, 32, part)
+            if d[2] == 0:
+                out.append(rcopy(frame.at[src + (slice(0, 128),)], frame.at[dst + (slice(0, 128),)], base + k, d))
+            else:
+                rows = slice(src[1].start - 8, src[1].stop - 8)
+                zr = zh0 if d[2] > 0 else zl0
+                out.append(rcopy(zs0.at[q, 1 if d[2] > 0 else 0, rows], zr.at[q, 1 - d[0], dst[1]], base + k, d))
+        return out
+
+    def late_copies():
+        out = []
+        for k, d in enumerate(XY_DIRS):
+            src, dst = frame_slices(d, 16, 6, 32, (3, 5))
+            out.append(rcopy(ff.at[src + (slice(0, 128),)], ff.at[dst + (slice(0, 128),)], SEM_LATE + k, d))
+        return out
+
+    def copies1(q, base, part):
+        out = []
+        for k, d in enumerate(DIRS):
+            src, dst = frame_slices(d, 8, 4, 16, part)
+            if d[2] == 0:
+                out.append(rcopy(f1.at[(q,) + src], f1.at[(q,) + dst], base + k, d))
+            else:
+                rows = slice(src[1].start - 8, src[1].stop - 8)
+                zr = zh1 if d[2] > 0 else zl1
+                out.append(rcopy(zs1.at[q, rows], zr.at[q, 1 - d[0], dst[1]], base + k, d))
+        return out
+
+    def copies2(q, base):
+        mine = t2.at[q, 1, 1, 8:16]
+        return [
+            rcopy(mine, t2.at[q, 1 - d[2], 1 - d[0], 8 * (1 - d[1]) : 8 * (1 - d[1]) + 8], base + k, d)
+            for k, d in enumerate(DIRS)
+        ]
+
+    def copies3a(q, base):
+        return [rcopy(x1.at[q, 0], x1.at[q, k + 1], base + k, (n, 0, 0)) for k, n in enumerate(X_NEAR)]
+
+    def copies3b(q, base):
+        return [
+            rcopy(y1.at[q, 1, 8:16], y1.at[q, 1 - d[2], 8 * (1 - d[1]) : 8 * (1 - d[1]) + 8], base + k, d)
+            for k, d in enumerate(YZ_NEAR)
+        ]
+
+    def copies4a(q, base):
+        return [rcopy(xa.at[q, gx], xa.at[q, gx], base + k, (n, 0, 0)) for k, n in enumerate(RING)]
+
+    def copies4b(q, base):
+        return [rcopy(yb.at[q, gy], yb.at[q, gy], base + k, (0, n, 0)) for k, n in enumerate(RING)]
+
+    def start(copies):
+        for item in copies:
+            item.start()
+
+    def wait_recv(copies):
+        for item in copies:
+            item.wait_recv()
+
+    def wait_send(copies):
+        for item in copies:
+            item.wait_send()
+
+    def in_x(i):
+        x = 16 * gx + i - 6
+        return jnp.where((x >= 0) & (x < 128), 1.0, 0.0)
+
+    def unpack0(frame, q, halo, own):
+        lane = iota((48, 128), 1)
+        keep = (lane < 8) | (lane >= 120)
+
+        def beside(slot, sx, i):
+            t = jnp.where((lane >= 8 * sx) & (lane < 8 * sx + 8), zl0[q, slot], zh0[q, slot])
+            t = pltpu.roll(t, lax.rem(128 - 8 * sx, 128), 1)
+            return jnp.where(keep, t, 0.0) * (k0[:, 128:256] * in_x(i))
+
+        for i in halo:
+            below = i < 6
+            frame[i, :, 0:128] = frame[i, :, 0:128] * (k0[:, 0:128] * in_x(i))
+            frame[i, :, 128:256] = beside(0 if below else 2, jnp.int32(i + 10 if below else i - 22), i)
+
+        def body(k, carry):
+            values = [(i, beside(1, i - 6, i)) for i in [4 * k + 6 + j for j in range(4)]]
+            for i, value in values:
+                frame[i, :, 128:256] = value
+                for rows in (slice(0, 8), slice(40, 48)):
+                    frame[i, rows, 0:128] = frame[i, rows, 0:128] * k0[rows, 0:128]
+            return carry
+
+        if own:
+            lax.fori_loop(0, 4, body, 0)
+
+    def unpack1(q):
+        lane = iota((32, 128), 1)
+        for i in range(16) if not isinstance(q, int) else range(3, 13):
+            slot = 0 if i < 4 else 1 if i < 12 else 2
+            sx = (4 + i) % 8 if i < 4 else (i - 4) % 8
+            lo = zl1[q, slot]
+            hi = zh1[q, slot]
+            if (64 - 16 * sx) % 128:
+                lo = pltpu.roll(lo, (64 - 16 * sx) % 128, 1)
+            if (112 - 16 * sx) % 128:
+                hi = pltpu.roll(hi, (112 - 16 * sx) % 128, 1)
+            t = jnp.where(lane < 64, f1[q, i], jnp.where(lane < 72, lo, jnp.where(lane >= 120, hi, 0.0)))
+            f1[q, i] = t * k1[i]
+
+    def unpack2(q):
+        lane = iota((24, 128), 1)
+        for i in range(12):
+            slot, sx = i // 4, i % 4
+            below, mid, above = t2[q, 0, slot], t2[q, 1, slot], t2[q, 2, slot]
+            if sx:
+                mid = pltpu.roll(mid, 128 - 32 * sx, 1)
+            if sx != 1:
+                above = pltpu.roll(above, (32 - 32 * sx) % 128, 1)
+            if sx != 3:
+                below = pltpu.roll(below, 96 - 32 * sx, 1)
+            t = jnp.where(lane < 32, mid, jnp.where(lane < 64, above, jnp.where(lane >= 96, below, 0.0)))
+            f2[i] = t * k2[i]
+
+    def unpack3(q):
+        lane = iota((24, 128), 1)
+        for dx in range(-2, 3):
+            shift = 16 * lax.rem(gx + (dx + 8), 8)
+
+            def turned(slot, target):
+                return pltpu.roll(y1[q, slot], lax.rem(128 + target - shift, 128), 1)
+
+            t = jnp.where(lane < 16, turned(1, 0), 0.0)
+            t = jnp.where((lane >= 16) & (lane < 32), turned(2, 16), t)
+            t = jnp.where(lane >= 112, turned(0, 112), t)
+            for y in range(3):
+                for x in range(2):
+                    f3[2 * dx + 4 + x, 4 + 4 * y : 8 + 4 * y, :] = t[8 * y + 4 * x : 8 * y + 4 * x + 4]
+        f3[...] = f3[...] * k3[...]
+
+    def unpack4(q):
+        lane = iota((64, 128), 1)
+        for y in range(2):
+            t = pltpu.roll(yb[q].reshape(64, 128), 120 - 32 * y, 1)
+            ts[y] = jnp.where((lane < 16) | (lane >= 120), t, 0.0)
+        for x in range(8):
+            for y in range(2):
+                f4[x, pl.ds(8 + y, 8, 2), :] = ts[y, pl.ds(x, 8, 8), :]
+
+    def prolong0(source, first, add):
+        es0[...] = mm(source.reshape(512, 128), prolong_matrix(128, 96, 256, 192)).reshape(16, 32, 256)
+
+        def rows(k, carry):
+            values = []
+            for i in (first + 2 * k, first + 2 * k + 1):
+                mid = 0.75 * es0[i, 4:28, :]
+                even = (mid + 0.25 * es0[i, 3:27, :]) * ke[...]
+                odd = (mid + 0.25 * es0[i, 5:29, :]) * ko[...]
+                values.append((i, even, odd))
+            for i, even, odd in values:
+                ye0[i] = even
+                yo0[i] = odd
+            return carry
+
+        lax.fori_loop(0, 8 - first, rows, 0)
+
+        def planes(step, carry):
+            for k in (first + 2 * step, first + 2 * step + 1):
+                for x, pair_of in enumerate(plane_pair(ye0, yo0, 1, k)):
+                    i = 2 * k + x
+                    for y, value in enumerate(pair_of):
+                        value = value * in_x(i)
+                        for h in range(2):
+                            at_rows = (h, i, pl.ds(y, 24, 2))
+                            part = value[:, 128 * h : 128 * h + 128]
+                            v1[at_rows] = v1[at_rows] + part if add else part
+            return carry
+
+        lax.fori_loop(0, 7 - first, planes, 0)
+
+    rho_copies = copies1(0, SEM_RHO, (0, 1))
+    start(rho_copies)
     hi_prec = lax.Precision.HIGHEST
     m = iota((9, 128), 0)
     c = iota((9, 128), 1)
@@ -196,221 +407,10 @@
     tp[10:13, 0:16] = corners + 5.5 + offset_t[...]
     tp[13:16, 0:16] = corners
     at[0:16, :] = packed + tp[...].T[0:16]
-    rho_in.wait()
-    f1[0, 4:12, 8:24, 0:64] = rho[...]
-    pack1(0)
+    atoms = atom_copies()
+    start(atoms)
     v0_in.wait()
     pack0(vf, 0)
-
-    pl.semaphore_wait(barrier, len(reached))
-
-    def rcopy(src, dst, k, d):
-        return pltpu.make_async_remote_copy(
-            src_ref=src, dst_ref=dst, send_sem=ss.at[k], recv_sem=rs.at[k], device_id=peer(d), device_id_type=MESH
-        )
-
-    def atom_copies():
-        return [
-            rcopy(at.at[0:16], at.at[16 * k + 16 : 16 * k + 32], k, d) for k, d in enumerate(UP7)
-        ]
-
-    def frame_slices(d, nx, hx, ny, part):
-        near, far = part
-        src, dst = [], []
-        for s, n, h, o, a, b in ((d[0], nx, hx, hx, near, far), (d[1], ny, 8, 8, 0, 8)):
-            if s == 0:
-                src.append(slice(o, o + n))
-                dst.append(slice(o, o + n))
-            elif s > 0:
-                src.append(slice(o + n - b, o + n - a))
-                dst.append(slice(h - b, h - a))
-            else:
-                src.append(slice(o + a, o + b))
-                dst.append(slice(o + n + a, o + n + b))
-        return tuple(src), tuple(dst)
-
-    def copies0(frame, q, base, part):
-        out = []
-        for k, d in enumerate(DIRS):
-            src, dst = frame_slices(d, 16, 6, 32, part)
-            if d[2] == 0:
-                out.append(rcopy(frame.at[src + (slice(0, 128),)], frame.at[dst + (slice(0, 128),)], base + k, d))
-            else:
-                rows = slice(src[1].start - 8, src[1].stop - 8)
-                zr = zh0 if d[2] > 0 else zl0
-                out.append(rcopy(zs0.at[q, 1 if d[2] > 0 else 0, rows], zr.at[q, 1 - d[0], dst[1]], base + k, d))
-        return out
-
-    def late_copies():
-        out = []
-        for k, d in enumerate(XY_DIRS):
-            src, dst = frame_slices(d, 16, 6, 32, (3, 5))
-            out.append(rcopy(ff.at[src + (slice(0, 128),)], ff.at[dst + (slice(0, 128),)], SEM_LATE + k, d))
-        return out
-
-    def copies1(q, base, part):
-        out = []
-        for k, d in enumerate(DIRS):
-            src, dst = frame_slices(d, 8, 4, 16, part)
-            if d[2] == 0:
-                out.append(rcopy(f1.at[(q,) + src], f1.at[(q,) + dst], base + k, d))
-            else:
-                rows = slice(src[1].start - 8, src[1].stop - 8)
-                zr = zh1 if d[2] > 0 else zl1
-                out.append(rcopy(zs1.at[q, rows], zr.at[q, 1 - d[0], dst[1]], base + k, d))
-        return out
-
-    def copies2(q, base):
-        mine = t2.at[q, 1, 1, 8:16]
-        return [
-            rcopy(mine, t2.at[q, 1 - d[2], 1 - d[0], 8 * (1 - d[1]) : 8 * (1 - d[1]) + 8], base + k, d)
-            for k, d in enumerate(DIRS)
-        ]
-
-    def copies3a(q, base):
-        return [rcopy(x1.at[q, 0], x1.at[q, k + 1], base + k, (n, 0, 0)) for k, n in enumerate(X_NEAR)]
-
-    def copies3b(q, base):
-        return [
-            rcopy(y1.at[q, 1, 8:16], y1.at[q, 1 - d[2], 8 * (1 - d[1]) : 8 * (1 - d[1]) + 8], base + k, d)
-            for k, d in enumerate(YZ_NEAR)
-        ]
-
-    def copies4a(q, base):
-        return [rcopy(xa.at[q, gx], xa.at[q, gx], base + k, (n, 0, 0)) for k, n in enumerate(RING)]
-
-    def copies4b(q, base):
-        return [rcopy(yb.at[q, gy], yb.at[q, gy], base + k, (0, n, 0)) for k, n in enumerate(RING)]
-
-    def start(copies):
-        for item in copies:
-            item.start()
-
-    def wait_recv(copies):
-        for item in copies:
-            item.wait_recv()
-
-    def wait_send(copies):
-        for item in copies:
-            item.wait_send()
-
-    def in_x(i):
-        x = 16 * gx + i - 6
-        return jnp.where((x >= 0) & (x < 128), 1.0, 0.0)
-
-    def unpack0(frame, q, halo, own):
-        lane = iota((48, 128), 1)
-        keep = (lane < 8) | (lane >= 120)
-
-        def beside(slot, sx, i):
-            t = jnp.where((lane >= 8 * sx) & (lane < 8 * sx + 8), zl0[q, slot], zh0[q, slot])
-            t = pltpu.roll(t, lax.rem(128 - 8 * sx, 128), 1)
-            return jnp.where(keep, t, 0.0) * (k0[:, 128:256] * in_x(i))
-
-        for i in halo:
-            below = i < 6
-            frame[i, :, 0:128] = frame[i, :, 0:128] * (k0[:, 0:128] * in_x(i))
-            frame[i, :, 128:256] = beside(0 if below else 2, jnp.int32(i + 10 if below else i - 22), i)
-
-        def body(k, carry):
-            values = [(i, beside(1, i - 6, i)) for i in [4 * k + 6 + j for j in range(4)]]
-            for i, value in values:
-                frame[i, :, 128:256] = value
-                for rows in (slice(0, 8), slice(40, 48)):
-                    frame[i, rows, 0:128] = frame[i, rows, 0:128] * k0[rows, 0:128]
-            return carry
-
-        if own:
-            lax.fori_loop(0, 4, body, 0)
-
-    def unpack1(q):
-        lane = iota((32, 128), 1)
-        for i in range(16) if not isinstance(q, int) else range(3, 13):
-            slot = 0 if i < 4 else 1 if i < 12 else 2
-            sx = (4 + i) % 8 if i < 4 else (i - 4) % 8
-            lo = zl1[q, slot]
-            hi = zh1[q, slot]
-            if (64 - 16 * sx) % 128:
-                lo = pltpu.roll(lo, (64 - 16 * sx) % 128, 1)
-            if (112 - 16 * sx) % 128:
-                hi = pltpu.roll(hi, (112 - 16 * sx) % 128, 1)
-            t = jnp.where(lane < 64, f1[q, i], jnp.where(lane < 72, lo, jnp.where(lane >= 120, hi, 0.0)))
-            f1[q, i] = t * k1[i]
-
-    def unpack2(q):
-        lane = iota((24, 128), 1)
-        for i in range(12):
-            slot, sx = i // 4, i % 4
-            below, mid, above = t2[q, 0, slot], t2[q, 1, slot], t2[q, 2, slot]
-            if sx:
-                mid = pltpu.roll(mid, 128 - 32 * sx, 1)
-            if sx != 1:
-                above = pltpu.roll(above, (32 - 32 * sx) % 128, 1)
-            if sx != 3:
-                below = pltpu.roll(below, 96 - 32 * sx, 1)
-            t = jnp.where(lane < 32, mid, jnp.where(lane < 64, above, jnp.where(lane >= 96, below, 0.0)))
-            f2[i] = t * k2[i]
-
-    def unpack3(q):
-        lane = iota((24, 128), 1)
-        for dx in range(-2, 3):
-            shift = 16 * lax.rem(gx + (dx + 8), 8)
-
-            def turned(slot, target):
-                return pltpu.roll(y1[q, slot], lax.rem(128 + target - shift, 128), 1)
-
-            t = jnp.where(lane < 16, turned(1, 0), 0.0)
-            t = jnp.where((lane >= 16) & (lane < 32), turned(2, 16), t)
-            t = jnp.where(lane >= 112, turned(0, 112), t)
-            for y in range(3):
-                for x in range(2):
-                    f3[2 * dx + 4 + x, 4 + 4 * y : 8 + 4 * y, :] = t[8 * y + 4 * x : 8 * y + 4 * x + 4]
-        f3[...] = f3[...] * k3[...]
-
-    def unpack4(q):
-        lane = iota((64, 128), 1)
-        for y in range(2):
-            t = pltpu.roll(yb[q].reshape(64, 128), 120 - 32 * y, 1)
-            ts[y] = jnp.where((lane < 16) | (lane >= 120), t, 0.0)
-        for x in range(8):
-            for y in range(2):
-                f4[x, pl.ds(8 + y, 8, 2), :] = ts[y, pl.ds(x, 8, 8), :]
-
-    def prolong0(source, first, add):
-        es0[...] = mm(source.reshape(512, 128), prolong_matrix(128, 96, 256, 192)).reshape(16, 32, 256)
-
-        def rows(k, carry):
-            values = []
-            for i in (first + 2 * k, first + 2 * k + 1):
-                mid = 0.75 * es0[i, 4:28, :]
-                even = (mid + 0.25 * es0[i, 3:27, :]) * ke[...]
-                odd = (mid + 0.25 * es0[i, 5:29, :]) * ko[...]
-                values.append((i, even, odd))
-            for i, even, odd in values:
-                ye0[i] = even
-                yo0[i] = odd
-            return carry
-
-        lax.fori_loop(0, 8 - first, rows, 0)
-
-        def planes(step, carry):
-            for k in (first + 2 * step, first + 2 * step + 1):
-                for x, pair_of in enumerate(plane_pair(ye0, yo0, 1, k)):
-                    i = 2 * k + x
-                    for y, value in enumerate(pair_of):
-                        value = value * in_x(i)
-                        for h in range(2):
-                            at_rows = (h, i, pl.ds(y, 24, 2))
-                            part = value[:, 128 * h : 128 * h + 128]
-                            v1[at_rows] = v1[at_rows] + part if add else part
-            return carry
-
-        lax.fori_loop(0, 7 - first, planes, 0)
-
-    atoms = atom_copies()
-    start(atoms)
-    rho_copies = copies1(0, SEM_RHO, (0, 1))
-    start(rho_copies)
     v_copies = copies0(vf, 0, SEM_V, (0, 6))
     start(v_copies)
 
@@ -547,7 +547,6 @@
         t2[q, 1, 1, 8:16] = 0.125 * mm(parts, m2)
         start(c2)
         pack1(q + 1)
-        start(c1)
 
         wait_recv(c2)
         unpack2(q)
@@ -570,10 +569,8 @@
         tile = jnp.concatenate([g3[1, 4:8, :], g3[2, 4:8, :]], axis=0)
         x1[q, 0] = pltpu.roll(jnp.where(iota((8, 128), 1) < 16, tile, 0.0), 16 * gx, 1)
         start(c3a)
+        start(c1)
         wait_send(c2)
-        wait_send(c1)
-        wait_recv(c1)
-        unpack1(q + 1)
         wait_recv(c4a)
         yb[q, gy] = xa[q].reshape(8, 128)
         start(c4b)
@@ -595,6 +592,9 @@
             pre(1, 2)
             pre(25, 2)
 
+        wait_send(c1)
+        wait_recv(c1)
+        unpack1(q + 1)
         wait_recv(c3b)
         unpack3(q)
         wait_recv(c4b)

time: 74.9 us -> 74.5 us (level)
  no operation moved by 1% of the time
where the time goes in v5:
time: 74.5 us; the launch traced here: 74.4 us
  Pallas kernels  71.8 us (96%)
  other arithmetic  1.96 us (3%)
    pallas_call x1, Pallas kernels, per_device(): pl.pallas_call(kernel, out_shape=(block, block, block), in_specs=[hbm] *...  71.8 us
    add x1, other arithmetic, per_device(): return (total_density, sweep + ALPHA * total_density)  1.96 us

profile of v5, /device:TPU:1, one launch (start us, length us, event | category | flops | bytes accessed | tf_op | source)
XLA Modules:
  0.0 74.4 jit_solution(8653965609264611411)
XLA Ops:
  0.6 71.8 %shard_map.77 = (f32[16,32,128]{2,1,0:T(8,128)}, f32[16,32,128]{2,1,0:T(8,128)}, f32[16,32,128]{2,1,0:T(8,128)}) custom-call(f32[8,16,64]{2,1,0:T(8,128)} %rho_hbm.1, f32[16,32,128]{2,1,0:T(8,128)} %v0_hbm.1, f32[16,91]{1,0:T(8,128)} %pair_hbm.1, f32[9,91]{1,0:T(8,128)} %bitcast.3, s32[3,16]{1,0:T(4,128)} %bitcast.4, f32[3,16]{1,0:T(4,128)} %bitcast.5), custom_call_target="tpu_custom_call" | custom-call | tf_op jit(solution)/shard_map/pallas_call | solution.py:693
  72.4 2.0 %multiply_add_fusion = (f32[16,32,128]{2,1,0:T(8,128)}, f32[16,32,128]{2,1,0:T(8,128)}) fusion(f32[16,32,128]{2,1,0:T(8,128)} %get-tuple-element.7, f32[16,32,128]{2,1,0:T(8,128)} %get-tuple-element.5, f32[16,32,128]{2,1,0:T(8,128)} %get-tuple-element.6), kind=kLoop, calls=%fused_computation | loop fusion | flops 196608 | bytes 1310720 | tf_op jit(solution)/shard_map/add | solution.py:704
